TPU v7x, 256 devices: a whole 4x4x8 slice. The times are simulated.
256 devices in a mesh: user: 16 (over z_hi, y, core), item: 4 (over x), hot: 4 (over z_lo).
Axes of the slice: x: 4, y: 4, z: 8 (z_hi: 2, z_lo: 4; z = z_hi * 4 + z_lo), core: 2. Of those that a mesh axis runs over, the one named last changes fastest.
Arguments:
- user_final: float32 [32768, 256], P(('user', 'item', 'hot')), may hold values from -1.5 to 1.5
- item_final: float32 [4096, 256], P(('user', 'item', 'hot')), may hold values from -1.5 to 1.5
- tiles: float32 [12288, 128, 128], P(('user', 'item', 'hot')), may hold values from 0 to 1
- tile_rows: int32 [12288], P(('user', 'item', 'hot')), may hold values from 0 to 15, as said below
- tile_cols: int32 [12288], P(('user', 'item', 'hot')), may hold values from 0 to 7
- tile_count: int32 [256], P(('user', 'item', 'hot')), may hold values from 1 to 48, as said below
- triplets: int32 [65536, 3], P(('user', 'item', 'hot')), may hold values from 0 to 32767, as said below
Outputs:
- user_grad: float32 [32768, 256], P(('user', 'item', 'hot'))
- item_grad: float32 [4096, 256], P(('user', 'item', 'hot'))
Inputs may be any that keep to these rules, and one draw needn't show every extreme that they name: `tile_count`: every device has at least one live slot; some device has exactly 1 and some exactly 48. `triplets`: rows r to r + 255 with r = d * 256 belong to device d; their users lie in that device's user block and both of their items in its item block. Column 0 holds users, columns 1 and 2 hold items. `tile_rows`: A device holds no tile position twice. Its slot s holds a tile whose row t satisfies (t // (16 / (4 * 4))) % 4 = s // (48 / 4).
All inputs are finite; a program needn't handle non-finite values.
Results may differ from a plain program's by a relative error of at most 0.0003.
Values sent between devices are 32-bit elements; how exact they have to be, the bound alone decides.
A program may use at most 64 MiB of HBM per device.

v0:
```python
import jax
import jax.numpy as jnp
from jax import lax
from jax.sharding import PartitionSpec as P

LAYERS = 2


def body(user_final, item_final, tiles, tile_rows, tile_cols, tile_count, triplets):
    highest = lax.Precision.HIGHEST
    user_share = user_final.shape[0]
    item_share = item_final.shape[0]
    width = user_final.shape[1]
    slot_total = tiles.shape[0]
    tile_size = tiles.shape[1]
    user_ways = lax.axis_size("user")
    item_ways = lax.axis_size("item")
    hot_ways = lax.axis_size("hot")
    block_users = user_share * item_ways * hot_ways
    block_items = item_share * user_ways * hot_ways
    user_tiles = block_users // tile_size
    item_tiles = block_items // tile_size
    users_block = lax.all_gather(user_final, ("item", "hot"), axis=0, tiled=True)
    items_block = lax.all_gather(item_final, ("user", "hot"), axis=0, tiled=True)
    local_buyers = triplets[:, 0] - lax.axis_index("user") * block_users

    def item_local(global_row):
        quotient = global_row // item_share
        inner_part = global_row % item_share
        hot_part = quotient % hot_ways
        outer_part = quotient // (hot_ways * item_ways)
        return (outer_part * hot_ways + hot_part) * item_share + inner_part

    local_chosen = item_local(triplets[:, 1])
    local_others = item_local(triplets[:, 2])
    buyer_rows = users_block[local_buyers]
    chosen_rows = items_block[local_chosen]
    other_rows = items_block[local_others]
    margin = jnp.sum(buyer_rows * (chosen_rows - other_rows), axis=1)
    weight_t = -jax.nn.sigmoid(-margin)
    user_terms = (
        jnp.zeros((block_users, width), jnp.float32)
        .at[local_buyers]
        .add(weight_t[:, None] * (chosen_rows - other_rows))
    )
    item_terms = (
        jnp.zeros((block_items, width), jnp.float32)
        .at[local_chosen]
        .add(weight_t[:, None] * buyer_rows)
    )
    item_terms = item_terms.at[local_others].add(-weight_t[:, None] * buyer_rows)
    grad_users = lax.psum_scatter(user_terms, ("item", "hot"), scatter_dimension=0, tiled=True)
    grad_items = lax.psum_scatter(item_terms, ("user", "hot"), scatter_dimension=0, tiled=True)
    alive = (jnp.arange(slot_total, dtype=jnp.int32) < tile_count[0]).astype(jnp.float32)
    masked_tiles = tiles * alive[:, None, None]
    work_tiles, work_rows, work_cols = (masked_tiles, tile_rows, tile_cols)
    work_slots = work_tiles.shape[0]
    row_onehot = (work_rows[:, None] == jnp.arange(user_tiles, dtype=jnp.int32)[None, :]).astype(
        jnp.float32
    )
    col_onehot = (work_cols[:, None] == jnp.arange(item_tiles, dtype=jnp.int32)[None, :]).astype(
        jnp.float32
    )
    state_users = grad_users
    state_items = grad_items
    for section_index in range(LAYERS):
        user_whole = lax.all_gather(state_users, ("item", "hot"), axis=0, tiled=True)
        item_whole = lax.all_gather(state_items, ("user", "hot"), axis=0, tiled=True)
        item_pieces = item_whole.reshape(item_tiles, tile_size, width)[work_cols]
        user_pieces = user_whole.reshape(user_tiles, tile_size, width)[work_rows]
        to_users = jnp.einsum("str,srd->std", work_tiles, item_pieces, precision=highest)
        to_items = jnp.einsum("str,std->srd", work_tiles, user_pieces, precision=highest)
        propagate_user_block_sum = jnp.einsum(
            "su,sx->ux",
            row_onehot,
            to_users.reshape(work_slots, tile_size * width),
            precision=highest,
        ).reshape(user_tiles * tile_size, width)
        item_block_sum = jnp.einsum(
            "si,sx->ix",
            col_onehot,
            to_items.reshape(work_slots, tile_size * width),
            precision=highest,
        ).reshape(block_items, width)
        from_items = lax.psum_scatter(
            propagate_user_block_sum, ("item", "hot"), scatter_dimension=0, tiled=True
        )
        from_users = lax.psum_scatter(
            item_block_sum, ("user", "hot"), scatter_dimension=0, tiled=True
        )
        from_items, from_users = (from_items, from_users)
        state_users = grad_users + from_items
        state_items = grad_items + from_users
    return (state_users / (LAYERS + 1.0), state_items / (LAYERS + 1.0))


def solution(mesh):
    placed = (
        P(("user", "item", "hot"), None),
        P(("user", "item", "hot"), None),
        P(("user", "item", "hot"), None, None),
        P(("user", "item", "hot")),
        P(("user", "item", "hot")),
        P(("user", "item", "hot")),
        P(("user", "item", "hot"), None),
    )
    return jax.shard_map(
        body,
        mesh=mesh,
        in_specs=placed,
        out_specs=(P(("user", "item", "hot"), None), P(("user", "item", "hot"), None)),
        check_vma=False,
    )
```

profile of v0, /device:TPU:1, one launch (start us, length us, event | category | flops | bytes accessed | tf_op | source)
XLA Modules:
  0.0 1908.8 jit_solution(5865574015645096749)
XLA Ops:
  9.6 183.6 %all-gather.9.cloned.1.call-done = f32[1024,256]{1,0:T(8,128)} async-done(((f32[16,256]{1,0:T(8,128)}), f32[1024,256]{1,0:T(8,128)}) %all-gather.9.cloned.1.call-update) | async-done | bytes 1048592 | tf_op jit(solution)/shard_map/all_gather | solution.py:24
  197.6 79.9 %all-gather.7.cloned.1.call-done = f32[2048,256]{1,0:T(8,128)} async-done(((f32[128,256]{1,0:T(8,128)}), f32[2048,256]{1,0:T(8,128)}) %all-gather.7.cloned.1.call-update) | async-done | bytes 2097168 | tf_op jit(solution)/shard_map/all_gather | solution.py:23
  277.5 2.6 gather_fusion
  280.2 3.5 scatter_custom_fusion
  283.7 89.1 %reduce-scatter.7.cloned.1.call-done = f32[128,256]{1,0:T(8,128)} async-done(((f32[2048,256]{1,0:T(8,128)}), f32[128,256]{1,0:T(8,128)}) %reduce-scatter.7.cloned.1.call-update) | async-done | bytes 131088 | tf_op jit(solution)/shard_map/reduce_scatter | solution.py:52
  375.2 2.5 scatter_custom_fusion.2
  379.7 79.9 %all-gather.11.cloned.1.call-done = f32[2048,256]{1,0:T(8,128)} async-done(((f32[128,256]{1,0:T(8,128)}), f32[2048,256]{1,0:T(8,128)}) %all-gather.11.cloned.1.call-update) | async-done | bytes 2097168 | tf_op jit(solution)/shard_map/all_gather | solution.py:67
  459.6 5.4 gather_fusion.3
  465.0 8.2 fusion.6
  473.2 3.6 copy.15
  476.8 3.2 fusion.24
  482.5 242.9 %reduce-scatter.9.cloned.1.call-done = f32[16,256]{1,0:T(8,128)} async-done(((f32[1024,256]{1,0:T(8,128)}), f32[16,256]{1,0:T(8,128)}) %reduce-scatter.9.cloned.1.call-update) | async-done | bytes 16400 | tf_op jit(solution)/shard_map/reduce_scatter | solution.py:53
  725.5 258.0 %reduce-scatter.11.cloned.1.call-done = f32[16,256]{1,0:T(8,128)} async-done(((f32[1024,256]{1,0:T(8,128)}), f32[16,256]{1,0:T(8,128)}) %reduce-scatter.11.cloned.1.call-update) | async-done | bytes 16400 | tf_op jit(solution)/shard_map/reduce_scatter | solution.py:88
  985.2 179.8 %all-gather.15.cloned.1.call-done = f32[1024,256]{1,0:T(8,128)} async-done(((f32[16,256]{1,0:T(8,128)}), f32[1024,256]{1,0:T(8,128)}) %all-gather.15.cloned.1.call-update) | async-done | bytes 1048592 | tf_op jit(solution)/shard_map/all_gather | solution.py:68
  1165.0 4.8 gather_fusion.5
  1169.9 8.2 fusion.2
  1178.1 3.6 copy.17
  1181.7 3.6 fusion.25
  1185.2 2.7 reshape.64
  1188.5 162.6 %all-gather.13.cloned.1.call-done = f32[1024,256]{1,0:T(8,128)} async-done(((f32[16,256]{1,0:T(8,128)}), f32[1024,256]{1,0:T(8,128)}) %all-gather.13.cloned.1.call-update) | async-done | bytes 1048592 | tf_op jit(solution)/shard_map/all_gather | solution.py:68
  1351.1 4.8 gather_fusion.4
  1355.9 8.2 fusion.4
  1364.1 3.6 copy.16
  1367.7 3.6 fusion.26
  1371.3 2.7 reshape.61
  1374.1 64.8 %reduce-scatter.15.cloned.1.call-done = f32[128,256]{1,0:T(8,128)} async-done(((f32[2048,256]{1,0:T(8,128)}), f32[128,256]{1,0:T(8,128)}) %reduce-scatter.15.cloned.1.call-update) | async-done | bytes 131088 | tf_op jit(solution)/shard_map/reduce_scatter | solution.py:85
  1439.0 90.5 %reduce-scatter.13.cloned.1.call-done = f32[128,256]{1,0:T(8,128)} async-done(((f32[2048,256]{1,0:T(8,128)}), f32[128,256]{1,0:T(8,128)}) %reduce-scatter.13.cloned.1.call-update) | async-done | bytes 131088 | tf_op jit(solution)/shard_map/reduce_scatter | solution.py:85
  1531.4 85.1 %all-gather.17.cloned.1.call-done = f32[2048,256]{1,0:T(8,128)} async-done(((f32[128,256]{1,0:T(8,128)}), f32[2048,256]{1,0:T(8,128)}) %all-gather.17.cloned.1.call-update) | async-done | bytes 2097168 | tf_op jit(solution)/shard_map/all_gather | solution.py:67
  1616.4 5.2 gather_fusion.6
  1621.6 8.2 fusion
  1629.8 3.6 copy.18
  1636.9 263.6 %reduce-scatter.17.cloned.1.call-done = f32[16,256]{1,0:T(8,128)} async-done(((f32[1024,256]{1,0:T(8,128)}), f32[16,256]{1,0:T(8,128)}) %reduce-scatter.17.cloned.1.call-update) | async-done | bytes 16400 | tf_op jit(solution)/shard_map/reduce_scatter | solution.py:88
  (56 shorter events, 21.9 us)
Async XLA Ops:
  7.2 186.1 %all-gather.9.cloned.1.call-start = ((), (), s32[]{:S(2)}) async-start(), calls=%async_computation.7 | async-start | bytes 1064960 | tf_op jit(solution)/shard_map/all_gather | solution.py:24
  7.9 269.6 %all-gather.7.cloned.1.call-start = ((), (), s32[]{:S(2)}) async-start(), calls=%async_computation.6 | async-start | bytes 2228224 | tf_op jit(solution)/shard_map/all_gather | solution.py:23
  8.6 364.2 %reduce-scatter.7.cloned.1.call-start = ((), (), s32[]{:S(2)}) async-start(), calls=%async_computation.8 | async-start | bytes 2228224 | tf_op jit(solution)/shard_map/reduce_scatter | solution.py:52
  197.6 182.1 %copy-start.4 = (s32[48]{0:T(128)S(1)}, s32[48]{0:T(128)}, u32[]{:S(2)}) copy-start(s32[48]{0:T(128)} %param.10) | copy-start | bytes 580
  283.7 175.9 %all-gather.11.cloned.1.call-start = ((), (), s32[]{:S(2)}) async-start(), calls=%async_computation.10 | async-start | bytes 2228224 | tf_op jit(solution)/shard_map/all_gather | solution.py:67
  372.9 352.6 %reduce-scatter.9.cloned.1.call-start = ((), (), s32[]{:S(2)}) async-start(), calls=%async_computation.9 | async-start | bytes 1064960 | tf_op jit(solution)/shard_map/reduce_scatter | solution.py:53
  377.7 1.1 copy-start.1
  378.8 604.8 %reduce-scatter.11.cloned.1.call-start = ((), (), s32[]{:S(2)}) async-start(), calls=%async_computation.11 | async-start | bytes 1064960 | tf_op jit(solution)/shard_map/reduce_scatter | solution.py:88
  459.6 5.4 copy-start
  473.2 3.6 copy-start.5
  482.5 682.5 %all-gather.15.cloned.1.call-start = ((), (), s32[]{:S(2)}) async-start(), calls=%async_computation.14 | async-start | bytes 1064960 | tf_op jit(solution)/shard_map/all_gather | solution.py:68
  725.5 625.6 %all-gather.13.cloned.1.call-start = ((), (), s32[]{:S(2)}) async-start(), calls=%async_computation.12 | async-start | bytes 1064960 | tf_op jit(solution)/shard_map/all_gather | solution.py:68
  984.9 454.0 %reduce-scatter.15.cloned.1.call-start = ((), (), s32[]{:S(2)}) async-start(), calls=%async_computation.15 | async-start | bytes 2228224 | tf_op jit(solution)/shard_map/reduce_scatter | solution.py:85
  1188.0 341.4 %reduce-scatter.13.cloned.1.call-start = ((), (), s32[]{:S(2)}) async-start(), calls=%async_computation.13 | async-start | bytes 2228224 | tf_op jit(solution)/shard_map/reduce_scatter | solution.py:85
  1367.7 161.7 %copy-start.2 = (f32[128,256]{1,0:T(8,128)S(1)}, f32[128,256]{1,0:T(8,128)}, u32[]{:S(2)}) copy-start(f32[128,256]{1,0:T(8,128)} %reduce-scatter.7.cloned.1.call-done) | copy-start | bytes 393220
  1374.1 242.4 %all-gather.17.cloned.1.call-start = ((), (), s32[]{:S(2)}) async-start(), calls=%async_computation.16 | async-start | bytes 2228224 | tf_op jit(solution)/shard_map/all_gather | solution.py:67
  1531.2 369.2 %reduce-scatter.17.cloned.1.call-start = ((), (), s32[]{:S(2)}) async-start(), calls=%async_computation.17 | async-start | bytes 1064960 | tf_op jit(solution)/shard_map/reduce_scatter | solution.py:88
  1633.4 267.0 %copy-start.3 = (f32[16,256]{1,0:T(8,128)S(1)}, f32[16,256]{1,0:T(8,128)}, u32[]{:S(2)}) copy-start(f32[16,256]{1,0:T(8,128)} %reduce-scatter.9.cloned.1.call-done) | copy-start | bytes 49156
Sparse Core Ops, SparseCore 0:
  9.8 183.3 all-gather.8
  195.0 82.4 all-gather.6
  283.8 89.0 reduce-scatter.6
  374.5 85.0 all-gather.10
  462.0 263.4 reduce-scatter.8
  728.0 255.5 reduce-scatter.10
  985.4 179.6 all-gather.14
  1167.4 183.6 all-gather.12
  1353.6 85.2 reduce-scatter.14
  1441.3 88.0 reduce-scatter.12
  1531.3 85.1 all-gather.16
  1637.0 263.3 reduce-scatter.16
where the time goes:
time: 1920 us; the launch traced here: 1910 us
  waiting for transfers between devices  1780 us (93%)
  local copies, waits for them, and re-layouts  51.6 us (3%)
  matrix products  45.4 us (2%)
    reduce_scatter x2, waiting for transfers between devices, body(): lax.psum_scatter(item_block_sum, ('user', 'hot'), scatter_dimension=0, ti...  522 us
    all_gather x2, waiting for transfers between devices, body(): lax.all_gather(state_items, ('user', 'hot'), axis=0, tiled=True)  342 us
    reduce_scatter x1, waiting for transfers between devices, body(): lax.psum_scatter(item_terms, ('user', 'hot'), scatter_dimension=0, tiled=...  243 us
    all_gather x1, waiting for transfers between devices, body(): lax.all_gather(item_final, ('user', 'hot'), axis=0, tiled=True)  184 us
    all_gather x2, waiting for transfers between devices, body(): lax.all_gather(state_users, ('item', 'hot'), axis=0, tiled=True)  165 us
    reduce_scatter x2, waiting for transfers between devices, body(): lax.psum_scatter(propagate_user_block_sum, ('item', 'hot'), scatter_dimen...  155 us
    reduce_scatter x1, waiting for transfers between devices, body(): lax.psum_scatter(user_terms, ('item', 'hot'), scatter_dimension=0, tiled=...  89.1 us
    all_gather x1, waiting for transfers between devices, body(): lax.all_gather(user_final, ('item', 'hot'), axis=0, tiled=True)  79.9 us
  transfers between devices with their start and end apart: 12, of which 12 were waited for; matrix products, arithmetic and copies ran while one was open for 4% of the time, Pallas kernels for 0%

commit v1 on v0

v1 whole, which is shorter than its diff:
```python
import jax
import jax.numpy as jnp
from jax import lax
from jax.experimental import pallas as pl
from jax.experimental.pallas import tpu as pltpu
from jax.sharding import PartitionSpec as P

MESH = pl.DeviceIdType.MESH
F32 = jnp.float32
BF16 = jnp.bfloat16
LAYERS = 2
ROUNDS = LAYERS + 1
GROUP = 12
PLACES = 32

U_AG, Z_AG, Y_AG, C_AG, C_RS, Y_RS, Z_RS, U_RS = 0, 3, 10, 13, 17, 21, 24, 31
PER_ROUND = 34
INTS = PER_ROUND * ROUNDS
TILES = INTS + 3
COPIES = TILES + 3


def split2(x):
    hi = x.astype(BF16)
    return hi, (x - hi.astype(F32)).astype(BF16)


def split3(x):
    hi = x.astype(BF16)
    rest = x - hi.astype(F32)
    mid = rest.astype(BF16)
    return hi, mid, (rest - mid.astype(F32)).astype(BF16)


def dot(a, b):
    return jnp.dot(a, b, preferred_element_type=F32)


def dot_nt(a, b):
    return lax.dot_general(a, b, (((1,), (1,)), ((), ())), preferred_element_type=F32)


def kernel(
    ints_ref,
    uf_ref,
    if_ref,
    tiles_ref,
    uo_ref,
    io_ref,
    gints,
    sints,
    tbuf,
    ah,
    al,
    ath,
    atl,
    ohu,
    ohd,
    ut,
    dt,
    wd,
    wu,
    ub,
    ib,
    pu,
    pi,
    um,
    ua,
    uz,
    rc,
    hb,
    ym,
    ya,
    yz,
    zs,
    zb,
    gu,
    gi,
    ssem,
    rsem,
    lsem,
):
    a = lax.axis_index("user")
    b = lax.axis_index("item")
    c = lax.axis_index("hot")
    core = a % 2
    y = (a // 2) % 4
    zhi = a // 8
    z = zhi * 4 + c

    def user_index(zhi_, y_, core_):
        return (zhi_ * 4 + y_) * 2 + core_

    def ring(v):
        even = v + 1 - 2 * (v % 2)
        odd = 3 - v
        first = (1 - core) * even + core * odd
        second = (1 - core) * odd + core * even
        return first, second, (v + 2) % 4

    x1, x2, xo = ring(b)
    y1, y2, yo = ring(y)
    ya_dev = (user_index(zhi, y1, core), b, c)
    yb_dev = (user_index(zhi, y2, core), b, c)
    xa_dev = (a, x1, c)
    xb_dev = (a, x2, c)
    sib = (user_index(zhi, y, 1 - core), b, c)

    def z_dev(k):
        other = (z + k) % 8
        return (user_index(other // 4, y, core), b, other % 4), other // 4, other % 4

    def hot_dev(k):
        other = (c + k) % 4
        return (a, b, other), other

    started = []

    def send(src, dst, index, dev):
        copy = pltpu.make_async_remote_copy(
            src_ref=src,
            dst_ref=dst,
            send_sem=ssem.at[index],
            recv_sem=rsem.at[index],
            device_id=dev,
            device_id_type=MESH,
        )
        copy.start()
        started.append(copy)

    def arrive(dst, index, dev):
        pltpu.make_async_remote_copy(
            src_ref=dst,
            dst_ref=dst,
            send_sem=ssem.at[index],
            recv_sem=rsem.at[index],
            device_id=dev,
            device_id_type=MESH,
        ).wait_recv()

    barrier = pltpu.get_barrier_semaphore()
    peers = [xa_dev, xb_dev, ya_dev, yb_dev, sib] + [z_dev(k)[0] for k in range(1, 8)]
    for dev in peers:
        pl.semaphore_signal(barrier, inc=1, device_id=dev, device_id_type=MESH)
    own_tiles = pltpu.make_async_copy(
        tiles_ref.at[pl.ds(c * GROUP, GROUP)], tbuf.at[c, pl.ds(0, GROUP)], lsem.at[0]
    )
    own_tiles.start()
    for h in range(4):
        tbuf[h, GROUP] = jnp.zeros((128, 128), F32)
    gints[c] = ints_ref[...]
    pl.semaphore_wait(barrier, len(peers))

    def gather_start(r, users, items):
        base = r * PER_ROUND
        ub[r, b] = users
        ib[r, zhi, y, core, pl.ds(pl.multiple_of(c * 16, 16), 16)] = items
        mine = ib.at[r, zhi, y, core, pl.ds(pl.multiple_of(c * 16, 16), 16)]
        for k in range(1, 8):
            send(mine, mine, base + Z_AG + k - 1, z_dev(k)[0])
        send(ub.at[r, b], ub.at[r, b], base + U_AG, xa_dev)
        send(ub.at[r, b], ub.at[r, b], base + U_AG + 1, xb_dev)

    def gather_users_forward(r):
        base = r * PER_ROUND
        arrive(ub.at[r, x1], base + U_AG, xa_dev)
        send(ub.at[r, x1], ub.at[r, x1], base + U_AG + 2, xb_dev)

    def gather_items_z(r):
        base = r * PER_ROUND
        for k in range(1, 8):
            dev, other_hi, other_lo = z_dev(8 - k)
            piece = ib.at[r, other_hi, y, core, pl.ds(pl.multiple_of(other_lo * 16, 16), 16)]
            arrive(piece, base + Z_AG + k - 1, dev)
        piece = ib.at[r, :, y, core]
        send(piece, piece, base + Y_AG, ya_dev)
        send(piece, piece, base + Y_AG + 1, yb_dev)
        send(piece, piece, base + C_AG, sib)

    def gather_items_y(r):
        base = r * PER_ROUND
        first = ib.at[r, :, y1, core]
        arrive(first, base + Y_AG, ya_dev)
        send(first, first, base + Y_AG + 2, yb_dev)
        send(first, first, base + C_AG + 1 + 2 * core, sib)
        second = ib.at[r, :, y2, core]
        arrive(second, base + Y_AG + 1, yb_dev)
        send(second, second, base + C_AG + 3 - 2 * core, sib)
        far = ib.at[r, :, yo, core]
        arrive(far, base + Y_AG + 2, yb_dev)
        send(far, far, base + C_AG + 2, sib)

    def gather_users_end(r):
        base = r * PER_ROUND
        arrive(ub.at[r, x2], base + U_AG + 1, xb_dev)
        arrive(ub.at[r, xo], base + U_AG + 2, xb_dev)

    def gather_items_end(r):
        base = r * PER_ROUND
        for k, other in ((0, y), (1, y + 1 - 2 * (y % 2)), (3, 3 - y), (2, yo)):
            arrive(ib.at[r, :, other, 1 - core], base + C_AG + k, sib)

    def scatter_items_core(r):
        base = r * PER_ROUND
        for k, other in ((2, yo), (1, y + 1 - 2 * (y % 2)), (3, 3 - y), (0, y)):
            send(pi.at[r, :, other, 1 - core], rc.at[r, :, other], base + C_RS + k, sib)

    def scatter_users_start(r):
        base = r * PER_ROUND
        send(pu.at[r, xo], um.at[r], base + U_RS, xb_dev)
        send(pu.at[r, x2], uz.at[r], base + U_RS + 1, xb_dev)

    def scatter_items_y(r):
        base = r * PER_ROUND

        def halves(k, other):
            arrive(rc.at[r, :, other], base + C_RS + k, sib)
            hb[r, other] = pi[r, :, other, core] + rc[r, :, other]

        halves(2, yo)
        send(hb.at[r, yo], ym.at[r], base + Y_RS, yb_dev)
        halves(1, y + 1 - 2 * (y % 2))
        halves(3, 3 - y)
        send(hb.at[r, y2], yz.at[r], base + Y_RS + 1, yb_dev)
        halves(0, y)

    def scatter_users_forward(r):
        base = r * PER_ROUND
        arrive(um.at[r], base + U_RS, xb_dev)
        pu[r, x1] = pu[r, x1] + um[r]
        send(pu.at[r, x1], ua.at[r], base + U_RS + 2, xa_dev)

    def scatter_items_z(r):
        base = r * PER_ROUND
        arrive(ym.at[r], base + Y_RS, yb_dev)
        hb[r, y1] = hb[r, y1] + ym[r]
        send(hb.at[r, y1], ya.at[r], base + Y_RS + 2, ya_dev)
        arrive(yz.at[r], base + Y_RS + 1, yb_dev)
        arrive(ya.at[r], base + Y_RS + 2, ya_dev)
        zs[r] = hb[r, y] + yz[r] + ya[r]
        for k in range(1, 8):
            dev, other_hi, other_lo = z_dev(k)
            send(
                zs.at[r, other_hi, pl.ds(pl.multiple_of(other_lo * 16, 16), 16)],
                zb.at[r, k - 1],
                base + Z_RS + k - 1,
                dev,
            )

    def scatter_users_end(r):
        base = r * PER_ROUND
        arrive(uz.at[r], base + U_RS + 1, xb_dev)
        arrive(ua.at[r], base + U_RS + 2, xa_dev)
        return pu[r, b] + uz[r] + ua[r]

    def scatter_items_end(r):
        base = r * PER_ROUND
        total = zs[r, zhi, pl.ds(pl.multiple_of(c * 16, 16), 16)]
        for k in range(1, 8):
            arrive(zb.at[r, k - 1], base + Z_RS + k - 1, z_dev(8 - k)[0])
            total = total + zb[r, k - 1]
        return total

    def store_items(r, m, value):
        first = 2 * m % 4
        pi[r, m // 2, first : first + 2] = value.reshape(2, 2, 64, 256)

    def scatter(r):
        scatter_items_y(r)
        scatter_users_forward(r)
        scatter_items_z(r)
        users = scatter_users_end(r)
        items = scatter_items_end(r)
        return users, items

    gather_start(0, uf_ref[...], if_ref[...])
    for k in range(1, 4):
        dev, other = hot_dev(k)
        send(gints.at[c], gints.at[c], INTS + k - 1, dev)
    for k in range(1, 4):
        dev, other = hot_dev(k)
        send(
            tiles_ref.at[pl.ds(other * GROUP, GROUP)],
            tbuf.at[c, pl.ds(0, GROUP)],
            TILES + k - 1,
            dev,
        )
    gather_users_forward(0)
    gather_items_z(0)
    for k in range(1, 4):
        dev, other = hot_dev(4 - k)
        arrive(gints.at[other], INTS + k - 1, dev)
    to_scalars = pltpu.make_async_copy(gints, sints, lsem.at[1])
    to_scalars.start()
    for h in range(4):
        span = slice(h * 256, (h + 1) * 256)
        buyers = jnp.where(gints[h, 1:2, :] == c, gints[h, 0:1, :], -1)
        rows = lax.broadcasted_iota(jnp.int32, (512, 256), 0)
        ohu[:, span] = jnp.where(rows == buyers, 1.0, 0.0).astype(BF16)
        rows = lax.broadcasted_iota(jnp.int32, (1024, 256), 0)
        chosen = jnp.where(rows == gints[h, 2:3, :], 1.0, 0.0)
        others = jnp.where(rows == gints[h, 3:4, :], 1.0, 0.0)
        ohd[:, span] = (chosen - others).astype(BF16)
    gather_items_y(0)
    gather_users_end(0)
    ut[0], ut[1], ut[2] = split3(ub[0].reshape(512, 256).T)
    gather_items_end(0)
    dt[0], dt[1], dt[2] = split3(ib[0].reshape(1024, 256).T)
    for h in range(4):
        span = slice(h * 256, (h + 1) * 256)
        buyer = dot(ut[0], ohu[:, span]) + dot(ut[1], ohu[:, span]) + dot(ut[2], ohu[:, span])
        differ = dot(dt[0], ohd[:, span]) + dot(dt[1], ohd[:, span]) + dot(dt[2], ohd[:, span])
        margin = jnp.sum(buyer * differ, axis=0, keepdims=True)
        small = jnp.exp(-jnp.abs(margin))
        coef = -jnp.where(margin >= 0, small, 1.0) / (1.0 + small)
        wu[0, :, span], wu[1, :, span] = split2(coef * buyer)
        wd[0, :, span], wd[1, :, span] = split2(coef * differ)
    for m in range(4):
        left = ohd[m * 256 : (m + 1) * 256, :]
        store_items(0, m, dot_nt(left, wu[0]) + dot_nt(left, wu[1]))
    scatter_items_core(0)
    pu[0] = (dot_nt(ohu[...], wd[0]) + dot_nt(ohu[...], wd[1])).reshape(4, 128, 256)
    scatter_users_start(0)
    users, items = scatter(0)
    gu[...] = users
    gi[...] = items

    for r in range(1, ROUNDS):
        gather_start(r, users, items)
        gather_users_forward(r)
        gather_items_z(r)
        gather_items_y(r)
        if r == 1:
            to_scalars.wait()
            own_tiles.wait()
            for k in range(1, 4):
                dev, other = hot_dev(4 - k)
                arrive(tbuf.at[other, pl.ds(0, GROUP)], TILES + k - 1, dev)

            def place(row, carry):
                at_row = pl.ds(pl.multiple_of(row * 128, 128), 128)
                for col in range(8):
                    at_col = slice(col * 128, (col + 1) * 128)
                    spot = c * PLACES + row * 8 + col
                    tile = tbuf[0, sints[0, 4, spot]]
                    for h in range(1, 4):
                        tile = tile + tbuf[h, sints[h, 4, spot]]
                    ah[at_row, at_col], al[at_row, at_col] = split2(tile)
                    ath[at_col, at_row], atl[at_col, at_row] = split2(tile.T)
                return carry

            lax.fori_loop(0, 4, place, 0)
        gather_users_end(r)
        uh, ul = split2(ub[r].reshape(512, 256))
        for m in range(4):
            rows = slice(m * 256, (m + 1) * 256)
            store_items(r, m, dot(ath[rows], uh) + dot(ath[rows], ul) + dot(atl[rows], uh))
        scatter_items_core(r)
        gather_items_end(r)
        xh, xl = split2(ib[r].reshape(1024, 256))
        pu[r] = (dot(ah[...], xh) + dot(ah[...], xl) + dot(al[...], xh)).reshape(4, 128, 256)
        scatter_users_start(r)
        users, items = scatter(r)
        users = gu[...] + users
        items = gi[...] + items

    uo_ref[...] = users / (LAYERS + 1.0)
    io_ref[...] = items / (LAYERS + 1.0)
    for copy in started:
        copy.wait_send()


def body(user_final, item_final, tiles, tile_rows, tile_cols, tile_count, triplets):
    slots = tiles.shape[0]
    buyers = triplets[:, 0] % 2048
    chosen = triplets[:, 1] // 256 * 64 + triplets[:, 1] % 64
    others = triplets[:, 2] // 256 * 64 + triplets[:, 2] % 64
    slot = jnp.arange(slots, dtype=jnp.int32)
    spot = slot // GROUP * PLACES + tile_rows // 4 * 8 + tile_cols
    spot = jnp.where(slot < tile_count[0], spot, -1)
    match = spot[None, :] == jnp.arange(4 * PLACES, dtype=jnp.int32)[:, None]
    source = GROUP + jnp.sum(jnp.where(match, slot % GROUP - GROUP, 0), axis=1)
    source = jnp.concatenate([source, source])
    blank = jnp.zeros_like(source)
    ints = jnp.stack(
        [
            buyers // 512 * 128 + buyers % 128,
            buyers // 128 % 4,
            chosen,
            others,
            source,
            blank,
            blank,
            blank,
        ]
    ).astype(jnp.int32)
    vmem = pl.BlockSpec(memory_space=pltpu.VMEM)
    return pl.pallas_call(
        kernel,
        out_shape=(
            jax.ShapeDtypeStruct((128, 256), F32),
            jax.ShapeDtypeStruct((16, 256), F32),
        ),
        in_specs=[vmem, vmem, vmem, pl.BlockSpec(memory_space=pl.ANY)],
        out_specs=(vmem, vmem),
        scratch_shapes=[
            pltpu.VMEM((4, 8, 256), jnp.int32),
            pltpu.SMEM((4, 8, 256), jnp.int32),
            pltpu.VMEM((4, GROUP + 1, 128, 128), F32),
            pltpu.VMEM((512, 1024), BF16),
            pltpu.VMEM((512, 1024), BF16),
            pltpu.VMEM((1024, 512), BF16),
            pltpu.VMEM((1024, 512), BF16),
            pltpu.VMEM((512, 1024), BF16),
            pltpu.VMEM((1024, 1024), BF16),
            pltpu.VMEM((3, 256, 512), BF16),
            pltpu.VMEM((3, 256, 1024), BF16),
            pltpu.VMEM((2, 256, 1024), BF16),
            pltpu.VMEM((2, 256, 1024), BF16),
            pltpu.VMEM((ROUNDS, 4, 128, 256), F32),
            pltpu.VMEM((ROUNDS, 2, 4, 2, 64, 256), F32),
            pltpu.VMEM((ROUNDS, 4, 128, 256), F32),
            pltpu.VMEM((ROUNDS, 2, 4, 2, 64, 256), F32),
            pltpu.VMEM((ROUNDS, 128, 256), F32),
            pltpu.VMEM((ROUNDS, 128, 256), F32),
            pltpu.VMEM((ROUNDS, 128, 256), F32),
            pltpu.VMEM((ROUNDS, 2, 4, 64, 256), F32),
            pltpu.VMEM((ROUNDS, 4, 2, 64, 256), F32),
            pltpu.VMEM((ROUNDS, 2, 64, 256), F32),
            pltpu.VMEM((ROUNDS, 2, 64, 256), F32),
            pltpu.VMEM((ROUNDS, 2, 64, 256), F32),
            pltpu.VMEM((ROUNDS, 2, 64, 256), F32),
            pltpu.VMEM((ROUNDS, 7, 16, 256), F32),
            pltpu.VMEM((128, 256), F32),
            pltpu.VMEM((16, 256), F32),
            pltpu.SemaphoreType.DMA((COPIES,)),
            pltpu.SemaphoreType.DMA((COPIES,)),
            pltpu.SemaphoreType.DMA((2,)),
        ],
        compiler_params=pltpu.CompilerParams(
            collective_id=0, has_side_effects=True, vmem_limit_bytes=52 * 1024 * 1024
        ),
        name="propagate",
    )(ints, user_final, item_final, tiles)


def solution(mesh):
    placed = (
        P(("user", "item", "hot"), None),
        P(("user", "item", "hot"), None),
        P(("user", "item", "hot"), None, None),
        P(("user", "item", "hot")),
        P(("user", "item", "hot")),
        P(("user", "item", "hot")),
        P(("user", "item", "hot"), None),
    )
    return jax.shard_map(
        body,
        mesh=mesh,
        in_specs=placed,
        out_specs=(P(("user", "item", "hot"), None), P(("user", "item", "hot"), None)),
        check_vma=False,
    )
```

time: 1920 us -> 161 us (0.08)
  waiting for transfers between devices: 1780 us -> 0 us
  Pallas kernels: 0 us -> 152 us
  local copies, waits for them, and re-layouts: 51.6 us -> 2.91 us
  matrix products: 45.4 us -> 0 us
    reduce_scatter x6 -> x0, waiting for transfers between devices: 1010 us -> none  [the longest x2 522 us: body(): lax.psum_scatter(item_block_sum, ('user', 'hot'), scatter_dimension=0, ti...]
    all_gather x6 -> x0, waiting for transfers between devices: 771 us -> none  [the longest x2 342 us: body(): lax.all_gather(state_items, ('user', 'hot'), axis=0, tiled=True)]
    pallas_call x0 -> x1, Pallas kernels: none -> 152 us  [body(): pl.pallas_call(kernel, out_shape=(jax.ShapeDtypeStruct((128, 256), F32),...]
    dot_general x8 -> x0, matrix products: 45.4 us -> none  [the longest x2 16.4 us: body(): jnp.einsum('str,srd->std', work_tiles, item_pieces, precision=highest)]
    gather x7 -> x0, local copies, waits for them, and re-layouts: 27.2 us -> none  [the longest x2 10.6 us: body(): user_pieces = user_whole.reshape(user_tiles, tile_size, width)[work_rows]]
  transfers between devices with their start and end apart: 12 -> 0, of which waited for: 12 -> 0; matrix products, arithmetic and copies ran while one was open for 4% -> 0% of each run, Pallas kernels for 0% -> 0%
where the time goes in v1:
time: 161 us; the launch traced here: 158 us
  Pallas kernels  152 us (94%)
  local copies, waits for them, and re-layouts  2.91 us (2%)
  other arithmetic  1.64 us (1%)
    pallas_call x1, Pallas kernels, body(): pl.pallas_call(kernel, out_shape=(jax.ShapeDtypeStruct((128, 256), F32),...  152 us

profile of v1, /device:TPU:1, one launch (start us, length us, event | category | flops | bytes accessed | tf_op | source)
XLA Modules:
  0.0 158.4 jit_solution(18258462020480254296)
XLA Ops:
  1.3 0.7 compare_select_fusion.4
  2.0 0.1 select_reduce_fusion
  2.1 0.8 and_select_fusion.4
  3.0 0.0 copy-start
  3.0 0.9 copy-done
  3.9 0.0 copy-start.1
  3.9 0.7 copy-done.1
  4.6 152.5 %propagate.1 = (f32[128,256]{1,0:T(8,128)S(1)}, f32[16,256]{1,0:T(8,128)S(1)}) custom-call(s32[8,256]{1,0:T(8,128)S(1)} %stack.15.ints_ref, f32[128,256]{1,0:T(8,128)S(1)} %copy-done, f32[16,256]{1,0:T(8,128)S(1)} %copy-done.1, f32[48,128,128]{2,1,0:T(8,128)} %tiles_ref.1), custom_call_target="tpu_custom_call" | custom-call | tf_op jit(solution)/shard_map/propagate/pallas_call | solution.py:398
  157.1 0.7 copy.12
  157.8 0.6 copy.13
  (6 shorter events, 0.1 us)
Async XLA Ops:
  3.0 0.9 copy-start
  3.9 0.7 copy-start.1

commit v2 on v1

--- a/solution.py
+++ b/solution.py
@@ -9,15 +9,17 @@
 F32 = jnp.float32
 BF16 = jnp.bfloat16
 LAYERS = 2
+
+
 ROUNDS = LAYERS + 1
 GROUP = 12
 PLACES = 32
 
-U_AG, Z_AG, Y_AG, C_AG, C_RS, Y_RS, Z_RS, U_RS = 0, 3, 10, 13, 17, 21, 24, 31
-PER_ROUND = 34
+U_AG, Z_AG, Y_AG, C_AG, C_RS, Y_RS, Z_RS, U_RS = 0, 7, 14, 17, 21, 25, 28, 35
+PER_ROUND = 42
 INTS = PER_ROUND * ROUNDS
 TILES = INTS + 3
-COPIES = TILES + 3
+COPIES = TILES + 2
 
 
 def split2(x):
@@ -49,7 +51,8 @@
     io_ref,
     gints,
     sints,
-    tbuf,
+    tbuf0,
+    tbuf1,
     ah,
     al,
     ath,
@@ -67,6 +70,7 @@
     um,
     ua,
     uz,
+    uq,
     rc,
     hb,
     ym,
@@ -104,6 +108,11 @@
     yb_dev = (user_index(zhi, y2, core), b, c)
     xa_dev = (a, x1, c)
     xb_dev = (a, x2, c)
+    tbuf = (tbuf0, tbuf1)
+    slot = c // 2
+    pair = c + 1 - 2 * (c % 2)
+    pair_dev = (a, b, pair)
+    far_dev = (a, b, (c + 2) % 4)
     sib = (user_index(zhi, y, 1 - core), b, c)
 
     def z_dev(k):
@@ -142,29 +151,47 @@
     peers = [xa_dev, xb_dev, ya_dev, yb_dev, sib] + [z_dev(k)[0] for k in range(1, 8)]
     for dev in peers:
         pl.semaphore_signal(barrier, inc=1, device_id=dev, device_id_type=MESH)
-    own_tiles = pltpu.make_async_copy(
-        tiles_ref.at[pl.ds(c * GROUP, GROUP)], tbuf.at[c, pl.ds(0, GROUP)], lsem.at[0]
-    )
-    own_tiles.start()
-    for h in range(4):
-        tbuf[h, GROUP] = jnp.zeros((128, 128), F32)
+    own_tiles = [
+        pltpu.make_async_copy(
+            tiles_ref.at[pl.ds((2 * h + c % 2) * GROUP, GROUP)],
+            tbuf[h].at[0, pl.ds(0, GROUP)],
+            lsem.at[h],
+        )
+        for h in range(2)
+    ]
+    for copy in own_tiles:
+        copy.start()
+    for h in range(2):
+        tbuf[h][0, GROUP] = jnp.zeros((128, 128), F32)
+        tbuf[h][1, GROUP] = jnp.zeros((128, 128), F32)
     gints[c] = ints_ref[...]
     pl.semaphore_wait(barrier, len(peers))
 
     def gather_start(r, users, items):
         base = r * PER_ROUND
-        ub[r, b] = users
         ib[r, zhi, y, core, pl.ds(pl.multiple_of(c * 16, 16), 16)] = items
         mine = ib.at[r, zhi, y, core, pl.ds(pl.multiple_of(c * 16, 16), 16)]
         for k in range(1, 8):
             send(mine, mine, base + Z_AG + k - 1, z_dev(k)[0])
-        send(ub.at[r, b], ub.at[r, b], base + U_AG, xa_dev)
-        send(ub.at[r, b], ub.at[r, b], base + U_AG + 1, xb_dev)
-
-    def gather_users_forward(r):
-        base = r * PER_ROUND
-        arrive(ub.at[r, x1], base + U_AG, xa_dev)
-        send(ub.at[r, x1], ub.at[r, x1], base + U_AG + 2, xb_dev)
+        ub[r, slot, b] = users
+        mine = ub.at[r, slot, b]
+        if r:
+            send(mine, mine, base + U_AG + 6, far_dev)
+        send(mine, mine, base + U_AG, xa_dev)
+        send(mine, mine, base + U_AG + 1, xb_dev)
+
+    def gather_users_far(r):
+        base = r * PER_ROUND + U_AG
+        other = ub.at[r, 1 - slot, b]
+        arrive(other, base + 6, far_dev)
+        send(other, other, base + 3, xa_dev)
+        send(other, other, base + 4, xb_dev)
+
+    def gather_users_forward(r, own):
+        base = r * PER_ROUND + U_AG + (0 if own else 3)
+        block = ub.at[r, slot if own else 1 - slot, x1]
+        arrive(block, base, xa_dev)
+        send(block, block, base + 2, xb_dev)
 
     def gather_items_z(r):
         base = r * PER_ROUND
@@ -190,10 +217,11 @@
         arrive(far, base + Y_AG + 2, yb_dev)
         send(far, far, base + C_AG + 2, sib)
 
-    def gather_users_end(r):
-        base = r * PER_ROUND
-        arrive(ub.at[r, x2], base + U_AG + 1, xb_dev)
-        arrive(ub.at[r, xo], base + U_AG + 2, xb_dev)
+    def gather_users_end(r, own):
+        base = r * PER_ROUND + U_AG + (0 if own else 3)
+        place = slot if own else 1 - slot
+        arrive(ub.at[r, place, x2], base + 1, xb_dev)
+        arrive(ub.at[r, place, xo], base + 2, xb_dev)
 
     def gather_items_end(r):
         base = r * PER_ROUND
@@ -205,10 +233,11 @@
         for k, other in ((2, yo), (1, y + 1 - 2 * (y % 2)), (3, 3 - y), (0, y)):
             send(pi.at[r, :, other, 1 - core], rc.at[r, :, other], base + C_RS + k, sib)
 
-    def scatter_users_start(r):
-        base = r * PER_ROUND
-        send(pu.at[r, xo], um.at[r], base + U_RS, xb_dev)
-        send(pu.at[r, x2], uz.at[r], base + U_RS + 1, xb_dev)
+    def scatter_users_start(r, own):
+        base = r * PER_ROUND + U_RS + 3 * own
+        place = slot if own else 1 - slot
+        send(pu.at[r, place, xo], um.at[r, own], base, xb_dev)
+        send(pu.at[r, place, x2], uz.at[r, own], base + 1, xb_dev)
 
     def scatter_items_y(r):
         base = r * PER_ROUND
@@ -224,11 +253,12 @@
         send(hb.at[r, y2], yz.at[r], base + Y_RS + 1, yb_dev)
         halves(0, y)
 
-    def scatter_users_forward(r):
-        base = r * PER_ROUND
-        arrive(um.at[r], base + U_RS, xb_dev)
-        pu[r, x1] = pu[r, x1] + um[r]
-        send(pu.at[r, x1], ua.at[r], base + U_RS + 2, xa_dev)
+    def scatter_users_forward(r, own):
+        base = r * PER_ROUND + U_RS + 3 * own
+        place = slot if own else 1 - slot
+        arrive(um.at[r, own], base, xb_dev)
+        pu[r, place, x1] = pu[r, place, x1] + um[r, own]
+        send(pu.at[r, place, x1], ua.at[r, own], base + 2, xa_dev)
 
     def scatter_items_z(r):
         base = r * PER_ROUND
@@ -247,11 +277,23 @@
                 dev,
             )
 
-    def scatter_users_end(r):
-        base = r * PER_ROUND
-        arrive(uz.at[r], base + U_RS + 1, xb_dev)
-        arrive(ua.at[r], base + U_RS + 2, xa_dev)
-        return pu[r, b] + uz[r] + ua[r]
+    def scatter_users_end(r, own):
+        base = r * PER_ROUND + U_RS + 3 * own
+        place = slot if own else 1 - slot
+        arrive(uz.at[r, own], base + 1, xb_dev)
+        arrive(ua.at[r, own], base + 2, xa_dev)
+        return pu[r, place, b] + uz[r, own] + ua[r, own]
+
+    def scatter_users_far(r):
+        pu[r, 1 - slot, b] = scatter_users_end(r, 0)
+        send(pu.at[r, 1 - slot, b], uq.at[r], r * PER_ROUND + U_RS + 6, far_dev)
+
+    def scatter_users_total(r):
+        total = scatter_users_end(r, 1)
+        if r:
+            arrive(uq.at[r], r * PER_ROUND + U_RS + 6, far_dev)
+            total = total + uq[r]
+        return total
 
     def scatter_items_end(r):
         base = r * PER_ROUND
@@ -266,104 +308,125 @@
         pi[r, m // 2, first : first + 2] = value.reshape(2, 2, 64, 256)
 
     def scatter(r):
+        if r:
+            scatter_users_forward(r, 0)
         scatter_items_y(r)
-        scatter_users_forward(r)
+        scatter_users_forward(r, 1)
+        if r:
+            scatter_users_far(r)
         scatter_items_z(r)
-        users = scatter_users_end(r)
+        users = scatter_users_total(r)
         items = scatter_items_end(r)
         return users, items
 
-    gather_start(0, uf_ref[...], if_ref[...])
-    for k in range(1, 4):
-        dev, other = hot_dev(k)
-        send(gints.at[c], gints.at[c], INTS + k - 1, dev)
-    for k in range(1, 4):
-        dev, other = hot_dev(k)
-        send(
-            tiles_ref.at[pl.ds(other * GROUP, GROUP)],
-            tbuf.at[c, pl.ds(0, GROUP)],
-            TILES + k - 1,
-            dev,
-        )
-    gather_users_forward(0)
-    gather_items_z(0)
-    for k in range(1, 4):
-        dev, other = hot_dev(4 - k)
-        arrive(gints.at[other], INTS + k - 1, dev)
-    to_scalars = pltpu.make_async_copy(gints, sints, lsem.at[1])
-    to_scalars.start()
-    for h in range(4):
-        span = slice(h * 256, (h + 1) * 256)
-        buyers = jnp.where(gints[h, 1:2, :] == c, gints[h, 0:1, :], -1)
-        rows = lax.broadcasted_iota(jnp.int32, (512, 256), 0)
-        ohu[:, span] = jnp.where(rows == buyers, 1.0, 0.0).astype(BF16)
-        rows = lax.broadcasted_iota(jnp.int32, (1024, 256), 0)
-        chosen = jnp.where(rows == gints[h, 2:3, :], 1.0, 0.0)
-        others = jnp.where(rows == gints[h, 3:4, :], 1.0, 0.0)
-        ohd[:, span] = (chosen - others).astype(BF16)
-    gather_items_y(0)
-    gather_users_end(0)
-    ut[0], ut[1], ut[2] = split3(ub[0].reshape(512, 256).T)
-    gather_items_end(0)
-    dt[0], dt[1], dt[2] = split3(ib[0].reshape(1024, 256).T)
-    for h in range(4):
-        span = slice(h * 256, (h + 1) * 256)
-        buyer = dot(ut[0], ohu[:, span]) + dot(ut[1], ohu[:, span]) + dot(ut[2], ohu[:, span])
-        differ = dot(dt[0], ohd[:, span]) + dot(dt[1], ohd[:, span]) + dot(dt[2], ohd[:, span])
-        margin = jnp.sum(buyer * differ, axis=0, keepdims=True)
-        small = jnp.exp(-jnp.abs(margin))
-        coef = -jnp.where(margin >= 0, small, 1.0) / (1.0 + small)
-        wu[0, :, span], wu[1, :, span] = split2(coef * buyer)
-        wd[0, :, span], wd[1, :, span] = split2(coef * differ)
-    for m in range(4):
-        left = ohd[m * 256 : (m + 1) * 256, :]
-        store_items(0, m, dot_nt(left, wu[0]) + dot_nt(left, wu[1]))
-    scatter_items_core(0)
-    pu[0] = (dot_nt(ohu[...], wd[0]) + dot_nt(ohu[...], wd[1])).reshape(4, 128, 256)
-    scatter_users_start(0)
-    users, items = scatter(0)
-    gu[...] = users
-    gi[...] = items
-
-    for r in range(1, ROUNDS):
+    def place_tiles(h):
+        own_tiles[h].wait()
+        arrive(tbuf[h].at[1, pl.ds(0, GROUP)], TILES + h, pair_dev)
+
+        def place(row, carry):
+            at_row = pl.ds(pl.multiple_of(h * 512 + row * 128, 128), 128)
+            for col in range(8):
+                at_col = slice(col * 128, (col + 1) * 128)
+                spot = (2 * h + c % 2) * PLACES + row * 8 + col
+                tile = tbuf[h][0, sints[c, 4, spot]] + tbuf[h][1, sints[pair, 4, spot]]
+                ah[at_row, at_col], al[at_row, at_col] = split2(tile)
+                ath[at_col, at_row], atl[at_col, at_row] = split2(tile.T)
+            return carry
+
+        lax.fori_loop(0, 4, place, 0)
+
+    to_scalars = pltpu.make_async_copy(gints, sints, lsem.at[2])
+
+    def loss_gradient():
+        gather_start(0, uf_ref[...], if_ref[...])
+        for k in range(1, 4):
+            dev, other = hot_dev(k)
+            send(gints.at[c], gints.at[c], INTS + k - 1, dev)
+        for h in range(2):
+            send(
+                tiles_ref.at[pl.ds((2 * h + 1 - c % 2) * GROUP, GROUP)],
+                tbuf[h].at[1, pl.ds(0, GROUP)],
+                TILES + h,
+                pair_dev,
+            )
+        gather_users_forward(0, 1)
+        gather_items_z(0)
+        for k in range(1, 4):
+            dev, other = hot_dev(4 - k)
+            arrive(gints.at[other], INTS + k - 1, dev)
+        to_scalars.start()
+        for h in range(4):
+            span = slice(h * 256, (h + 1) * 256)
+            buyers = jnp.where(gints[h, 1:2, :] == c, gints[h, 0:1, :], -1)
+            rows = lax.broadcasted_iota(jnp.int32, (512, 256), 0)
+            ohu[:, span] = jnp.where(rows == buyers, 1.0, 0.0).astype(BF16)
+            rows = lax.broadcasted_iota(jnp.int32, (1024, 256), 0)
+            chosen = jnp.where(rows == gints[h, 2:3, :], 1.0, 0.0)
+            others = jnp.where(rows == gints[h, 3:4, :], 1.0, 0.0)
+            ohd[:, span] = (chosen - others).astype(BF16)
+        gather_items_y(0)
+        gather_users_end(0, 1)
+        ut[0], ut[1], ut[2] = split3(ub[0, slot].reshape(512, 256).T)
+        gather_items_end(0)
+        dt[0], dt[1], dt[2] = split3(ib[0].reshape(1024, 256).T)
+        for h in range(4):
+            span = slice(h * 256, (h + 1) * 256)
+            hot, signed = ohu[:, span], ohd[:, span]
+            buyer = dot(ut[0], hot) + dot(ut[1], hot) + dot(ut[2], hot)
+            differ = dot(dt[0], signed) + dot(dt[1], signed) + dot(dt[2], signed)
+            margin = jnp.sum(buyer * differ, axis=0, keepdims=True)
+            small = jnp.exp(-jnp.abs(margin))
+            coef = -jnp.where(margin >= 0, small, 1.0) / (1.0 + small)
+            wu[0, :, span], wu[1, :, span] = split2(coef * buyer)
+            wd[0, :, span], wd[1, :, span] = split2(coef * differ)
+        for m in range(4):
+            left = ohd[m * 256 : (m + 1) * 256, :]
+            store_items(0, m, dot_nt(left, wu[0]) + dot_nt(left, wu[1]))
+        scatter_items_core(0)
+        sums = dot_nt(ohu[...], wd[0]) + dot_nt(ohu[...], wd[1])
+        pu[0, slot] = sums.reshape(4, 128, 256)
+        scatter_users_start(0, 1)
+        return scatter(0)
+
+    def layer(r, users, items):
         gather_start(r, users, items)
-        gather_users_forward(r)
-        gather_items_z(r)
-        gather_items_y(r)
         if r == 1:
             to_scalars.wait()
-            own_tiles.wait()
-            for k in range(1, 4):
-                dev, other = hot_dev(4 - k)
-                arrive(tbuf.at[other, pl.ds(0, GROUP)], TILES + k - 1, dev)
-
-            def place(row, carry):
-                at_row = pl.ds(pl.multiple_of(row * 128, 128), 128)
-                for col in range(8):
-                    at_col = slice(col * 128, (col + 1) * 128)
-                    spot = c * PLACES + row * 8 + col
-                    tile = tbuf[0, sints[0, 4, spot]]
-                    for h in range(1, 4):
-                        tile = tile + tbuf[h, sints[h, 4, spot]]
-                    ah[at_row, at_col], al[at_row, at_col] = split2(tile)
-                    ath[at_col, at_row], atl[at_col, at_row] = split2(tile.T)
-                return carry
-
-            lax.fori_loop(0, 4, place, 0)
-        gather_users_end(r)
-        uh, ul = split2(ub[r].reshape(512, 256))
+            place_tiles(0)
+        gather_users_far(r)
+        gather_users_forward(r, 1)
+        gather_items_z(r)
+        if r == 1:
+            place_tiles(1)
+        gather_users_forward(r, 0)
+        gather_items_y(r)
+        gather_users_end(r, 1)
+        gather_users_end(r, 0)
+        uh, ul = split2(ub[r].reshape(1024, 256))
         for m in range(4):
             rows = slice(m * 256, (m + 1) * 256)
             store_items(r, m, dot(ath[rows], uh) + dot(ath[rows], ul) + dot(atl[rows], uh))
         scatter_items_core(r)
         gather_items_end(r)
         xh, xl = split2(ib[r].reshape(1024, 256))
-        pu[r] = (dot(ah[...], xh) + dot(ah[...], xl) + dot(al[...], xh)).reshape(4, 128, 256)
-        scatter_users_start(r)
+        for own in range(2):
+            place = slot if own else 1 - slot
+            rows = pl.ds(pl.multiple_of(place * 512, 512), 512)
+            sums = dot(ah[rows], xh) + dot(ah[rows], xl) + dot(al[rows], xh)
+            pu[r, place] = sums.reshape(4, 128, 256)
+            scatter_users_start(r, own)
         users, items = scatter(r)
-        users = gu[...] + users
-        items = gi[...] + items
-
+        return gu[...] + users, gi[...] + items
+
+    def rounds():
+        users, items = loss_gradient()
+        gu[...] = users
+        gi[...] = items
+        for r in range(1, ROUNDS):
+            users, items = layer(r, users, items)
+        return users, items
+
+    users, items = rounds()
     uo_ref[...] = users / (LAYERS + 1.0)
     io_ref[...] = items / (LAYERS + 1.0)
     for copy in started:
@@ -406,23 +469,25 @@
         scratch_shapes=[
             pltpu.VMEM((4, 8, 256), jnp.int32),
             pltpu.SMEM((4, 8, 256), jnp.int32),
-            pltpu.VMEM((4, GROUP + 1, 128, 128), F32),
-            pltpu.VMEM((512, 1024), BF16),
-            pltpu.VMEM((512, 1024), BF16),
-            pltpu.VMEM((1024, 512), BF16),
-            pltpu.VMEM((1024, 512), BF16),
+            pltpu.VMEM((2, GROUP + 1, 128, 128), F32),
+            pltpu.VMEM((2, GROUP + 1, 128, 128), F32),
+            pltpu.VMEM((1024, 1024), BF16),
+            pltpu.VMEM((1024, 1024), BF16),
+            pltpu.VMEM((1024, 1024), BF16),
+            pltpu.VMEM((1024, 1024), BF16),
             pltpu.VMEM((512, 1024), BF16),
             pltpu.VMEM((1024, 1024), BF16),
             pltpu.VMEM((3, 256, 512), BF16),
             pltpu.VMEM((3, 256, 1024), BF16),
             pltpu.VMEM((2, 256, 1024), BF16),
             pltpu.VMEM((2, 256, 1024), BF16),
-            pltpu.VMEM((ROUNDS, 4, 128, 256), F32),
+            pltpu.VMEM((ROUNDS, 2, 4, 128, 256), F32),
             pltpu.VMEM((ROUNDS, 2, 4, 2, 64, 256), F32),
-            pltpu.VMEM((ROUNDS, 4, 128, 256), F32),
+            pltpu.VMEM((ROUNDS, 2, 4, 128, 256), F32),
             pltpu.VMEM((ROUNDS, 2, 4, 2, 64, 256), F32),
-            pltpu.VMEM((ROUNDS, 128, 256), F32),
-            pltpu.VMEM((ROUNDS, 128, 256), F32),
+            pltpu.VMEM((ROUNDS, 2, 128, 256), F32),
+            pltpu.VMEM((ROUNDS, 2, 128, 256), F32),
+            pltpu.VMEM((ROUNDS, 2, 128, 256), F32),
             pltpu.VMEM((ROUNDS, 128, 256), F32),
             pltpu.VMEM((ROUNDS, 2, 4, 64, 256), F32),
             pltpu.VMEM((ROUNDS, 4, 2, 64, 256), F32),
@@ -435,7 +500,7 @@
             pltpu.VMEM((16, 256), F32),
             pltpu.SemaphoreType.DMA((COPIES,)),
             pltpu.SemaphoreType.DMA((COPIES,)),
-            pltpu.SemaphoreType.DMA((2,)),
+            pltpu.SemaphoreType.DMA((3,)),
         ],
         compiler_params=pltpu.CompilerParams(
             collective_id=0, has_side_effects=True, vmem_limit_bytes=52 * 1024 * 1024

time: 161 us -> 143 us (0.89)
  Pallas kernels: 152 us -> 136 us
    pallas_call x1, Pallas kernels: 152 us -> 136 us  [body(): pl.pallas_call(kernel, out_shape=(jax.ShapeDtypeStruct((128, 256), F32),...]
where the time goes in v2:
time: 143 us; the launch traced here: 142 us
  Pallas kernels  136 us (95%)
  local copies, waits for them, and re-layouts  2.91 us (2%)
  other arithmetic  1.64 us (1%)
    pallas_call x1, Pallas kernels, body(): pl.pallas_call(kernel, out_shape=(jax.ShapeDtypeStruct((128, 256), F32),...  136 us
    unnamed x6, local copies, waits for them, and re-layouts  2.88 us

profile of v2, /device:TPU:1, one launch (start us, length us, event | category | flops | bytes accessed | tf_op | source)
XLA Modules:
  0.0 141.9 jit_solution(2269675876357998802)
XLA Ops:
  1.3 0.7 compare_select_fusion.4
  2.0 0.1 select_reduce_fusion
  2.1 0.8 and_select_fusion.4
  3.0 0.0 copy-start
  3.0 0.9 copy-done
  3.9 0.0 copy-start.1
  3.9 0.7 copy-done.1
  4.6 136.0 %propagate.1 = (f32[128,256]{1,0:T(8,128)S(1)}, f32[16,256]{1,0:T(8,128)S(1)}) custom-call(s32[8,256]{1,0:T(8,128)S(1)} %stack.15.ints_ref, f32[128,256]{1,0:T(8,128)S(1)} %copy-done, f32[16,256]{1,0:T(8,128)S(1)} %copy-done.1, f32[48,128,128]{2,1,0:T(8,128)} %tiles_ref.1), custom_call_target="tpu_custom_call" | custom-call | tf_op jit(solution)/shard_map/propagate/pallas_call | solution.py:461
  140.6 0.7 copy.12
  141.3 0.6 copy.13
  (6 shorter events, 0.1 us)
Async XLA Ops:
  3.0 0.9 copy-start
  3.9 0.7 copy-start.1

commit v3 on v2

--- a/solution.py
+++ b/solution.py
@@ -15,11 +15,26 @@
 GROUP = 12
 PLACES = 32
 
-U_AG, Z_AG, Y_AG, C_AG, C_RS, Y_RS, Z_RS, U_RS = 0, 7, 14, 17, 21, 25, 28, 35
-PER_ROUND = 42
+CHUNKS = 4
+CHUNK = 32
+PIECES = 6
+PIECE = 4
+EARLY = 4
+
+U_AG = 0
+Z_AG = U_AG + 7 * CHUNKS
+Y_AG = Z_AG + 7
+C_AG = Y_AG + 24
+C_RS = C_AG + 11
+Y_RS = C_RS + 4
+Z_RS = Y_RS + 24
+U_RS = Z_RS + 7
+PER_ROUND = U_RS + 7 * CHUNKS
 INTS = PER_ROUND * ROUNDS
 TILES = INTS + 3
-COPIES = TILES + 2
+COPIES = TILES + PIECES
+NEAR_FIRST = (1, 7, 2, 6, 3, 5, 4)
+FAR_FIRST = (4, 5, 3, 6, 2, 7, 1)
 
 
 def split2(x):
@@ -59,6 +74,7 @@
     atl,
     ohu,
     ohd,
+    buy,
     ut,
     dt,
     wd,
@@ -167,138 +183,182 @@
     gints[c] = ints_ref[...]
     pl.semaphore_wait(barrier, len(peers))
 
-    def gather_start(r, users, items):
-        base = r * PER_ROUND
-        ib[r, zhi, y, core, pl.ds(pl.multiple_of(c * 16, 16), 16)] = items
-        mine = ib.at[r, zhi, y, core, pl.ds(pl.multiple_of(c * 16, 16), 16)]
-        for k in range(1, 8):
-            send(mine, mine, base + Z_AG + k - 1, z_dev(k)[0])
+    def chunk(q):
+        return pl.ds(q * CHUNK, CHUNK)
+
+    def place_of(own):
+        return slot if own else 1 - slot
+
+    def along_z(k):
+        other = (z + k) % 8
+        return other // 4, other % 4
+
+    def gather_users_start(r, users):
+        base = r * PER_ROUND + U_AG
         ub[r, slot, b] = users
-        mine = ub.at[r, slot, b]
-        if r:
-            send(mine, mine, base + U_AG + 6, far_dev)
-        send(mine, mine, base + U_AG, xa_dev)
-        send(mine, mine, base + U_AG + 1, xb_dev)
+        for q in range(CHUNKS):
+            mine = ub.at[r, slot, b, chunk(q)]
+            if r:
+                send(mine, mine, base + 6 * CHUNKS + q, far_dev)
+            send(mine, mine, base + q, xa_dev)
+            send(mine, mine, base + CHUNKS + q, xb_dev)
 
     def gather_users_far(r):
         base = r * PER_ROUND + U_AG
-        other = ub.at[r, 1 - slot, b]
-        arrive(other, base + 6, far_dev)
-        send(other, other, base + 3, xa_dev)
-        send(other, other, base + 4, xb_dev)
+        for q in range(CHUNKS):
+            other = ub.at[r, 1 - slot, b, chunk(q)]
+            arrive(other, base + 6 * CHUNKS + q, far_dev)
+            send(other, other, base + 3 * CHUNKS + q, xa_dev)
+            send(other, other, base + 4 * CHUNKS + q, xb_dev)
 
     def gather_users_forward(r, own):
-        base = r * PER_ROUND + U_AG + (0 if own else 3)
-        block = ub.at[r, slot if own else 1 - slot, x1]
-        arrive(block, base, xa_dev)
-        send(block, block, base + 2, xb_dev)
-
-    def gather_items_z(r):
-        base = r * PER_ROUND
-        for k in range(1, 8):
-            dev, other_hi, other_lo = z_dev(8 - k)
-            piece = ib.at[r, other_hi, y, core, pl.ds(pl.multiple_of(other_lo * 16, 16), 16)]
-            arrive(piece, base + Z_AG + k - 1, dev)
-        piece = ib.at[r, :, y, core]
-        send(piece, piece, base + Y_AG, ya_dev)
-        send(piece, piece, base + Y_AG + 1, yb_dev)
-        send(piece, piece, base + C_AG, sib)
-
-    def gather_items_y(r):
-        base = r * PER_ROUND
-        first = ib.at[r, :, y1, core]
-        arrive(first, base + Y_AG, ya_dev)
-        send(first, first, base + Y_AG + 2, yb_dev)
-        send(first, first, base + C_AG + 1 + 2 * core, sib)
-        second = ib.at[r, :, y2, core]
-        arrive(second, base + Y_AG + 1, yb_dev)
-        send(second, second, base + C_AG + 3 - 2 * core, sib)
-        far = ib.at[r, :, yo, core]
-        arrive(far, base + Y_AG + 2, yb_dev)
-        send(far, far, base + C_AG + 2, sib)
+        base = r * PER_ROUND + U_AG + (0 if own else 3 * CHUNKS)
+        for q in range(CHUNKS):
+            block = ub.at[r, place_of(own), x1, chunk(q)]
+            arrive(block, base + q, xa_dev)
+            send(block, block, base + 2 * CHUNKS + q, xb_dev)
 
     def gather_users_end(r, own):
-        base = r * PER_ROUND + U_AG + (0 if own else 3)
-        place = slot if own else 1 - slot
-        arrive(ub.at[r, place, x2], base + 1, xb_dev)
-        arrive(ub.at[r, place, xo], base + 2, xb_dev)
+        base = r * PER_ROUND + U_AG + (0 if own else 3 * CHUNKS)
+        for q in range(CHUNKS):
+            arrive(ub.at[r, place_of(own), x2, chunk(q)], base + CHUNKS + q, xb_dev)
+        for q in range(CHUNKS):
+            arrive(ub.at[r, place_of(own), xo, chunk(q)], base + 2 * CHUNKS + q, xb_dev)
+
+    def scatter_users_start(r, own):
+        base = r * PER_ROUND + U_RS + 3 * CHUNKS * own
+        place = place_of(own)
+        for q in range(CHUNKS):
+            send(pu.at[r, place, xo, chunk(q)], um.at[r, own, chunk(q)], base + q, xb_dev)
+        for q in range(CHUNKS):
+            send(pu.at[r, place, x2, chunk(q)], uz.at[r, own, chunk(q)], base + CHUNKS + q, xb_dev)
+
+    def scatter_users_forward(r, own):
+        base = r * PER_ROUND + U_RS + 3 * CHUNKS * own
+        place = place_of(own)
+        for q in range(CHUNKS):
+            arrive(um.at[r, own, chunk(q)], base + q, xb_dev)
+            pu[r, place, x1, chunk(q)] = pu[r, place, x1, chunk(q)] + um[r, own, chunk(q)]
+            sums = pu.at[r, place, x1, chunk(q)]
+            send(sums, ua.at[r, own, chunk(q)], base + 2 * CHUNKS + q, xa_dev)
+
+    def scatter_users_sum(r, own):
+        base = r * PER_ROUND + U_RS + 3 * CHUNKS * own
+        place = place_of(own)
+        for q in range(CHUNKS):
+            arrive(uz.at[r, own, chunk(q)], base + CHUNKS + q, xb_dev)
+            arrive(ua.at[r, own, chunk(q)], base + 2 * CHUNKS + q, xa_dev)
+            sums = pu[r, place, b, chunk(q)] + uz[r, own, chunk(q)] + ua[r, own, chunk(q)]
+            pu[r, place, b, chunk(q)] = sums
+            if not own:
+                index = r * PER_ROUND + U_RS + 6 * CHUNKS + q
+                send(pu.at[r, place, b, chunk(q)], uq.at[r, chunk(q)], index, far_dev)
+
+    def scatter_users_total(r):
+        scatter_users_sum(r, 1)
+        total = pu[r, slot, b]
+        if r:
+            for q in range(CHUNKS):
+                arrive(uq.at[r, chunk(q)], r * PER_ROUND + U_RS + 6 * CHUNKS + q, far_dev)
+            total = total + uq[r]
+        return total
+
+    def gather_items_start(r, items):
+        base = r * PER_ROUND
+        ib[r, zhi, y, core, c] = items
+        mine = ib.at[r, zhi, y, core, c]
+        for k in FAR_FIRST:
+            send(mine, mine, base + Z_AG + k - 1, z_dev(k)[0])
+        send(mine, mine, base + Y_AG, ya_dev)
+        send(mine, mine, base + Y_AG + 8, yb_dev)
+
+    def gather_items_z(r, steps):
+        base = r * PER_ROUND
+        for k in steps:
+            hi, lo = along_z(k)
+            piece = ib.at[r, hi, y, core, lo]
+            arrive(piece, base + Z_AG + (8 - k) - 1, z_dev(k)[0])
+            send(piece, piece, base + Y_AG + k, ya_dev)
+            send(piece, piece, base + Y_AG + 8 + k, yb_dev)
+
+    def gather_items_forward(r, steps):
+        base = r * PER_ROUND
+        for k in steps:
+            hi, lo = along_z(k)
+            piece = ib.at[r, hi, y1, core, lo]
+            arrive(piece, base + Y_AG + k, ya_dev)
+            send(piece, piece, base + Y_AG + 16 + k, yb_dev)
+
+    def gather_items_core(r):
+        base = r * PER_ROUND
+        for index, other in ((0, y), (1 + core, y1)):
+            block = ib.at[r, :, other, core]
+            send(block, block, base + C_AG + index, sib)
+        for k in (0,) + NEAR_FIRST:
+            hi, lo = along_z(k)
+            arrive(ib.at[r, hi, y2, core, lo], base + Y_AG + 8 + k, yb_dev)
+        block = ib.at[r, :, y2, core]
+        send(block, block, base + C_AG + 2 - core, sib)
+        for k in (0,) + NEAR_FIRST:
+            hi, lo = along_z(k)
+            piece = ib.at[r, hi, yo, core, lo]
+            arrive(piece, base + Y_AG + 16 + k, yb_dev)
+            send(piece, piece, base + C_AG + 3 + k, sib)
 
     def gather_items_end(r):
         base = r * PER_ROUND
-        for k, other in ((0, y), (1, y + 1 - 2 * (y % 2)), (3, 3 - y), (2, yo)):
-            arrive(ib.at[r, :, other, 1 - core], base + C_AG + k, sib)
+        for index, other in ((0, y), (1, y + 1 - 2 * (y % 2)), (2, 3 - y)):
+            arrive(ib.at[r, :, other, 1 - core], base + C_AG + index, sib)
+        for k in (0,) + NEAR_FIRST:
+            hi, lo = along_z(k)
+            arrive(ib.at[r, hi, yo, 1 - core, lo], base + C_AG + 3 + k, sib)
 
     def scatter_items_core(r):
         base = r * PER_ROUND
         for k, other in ((2, yo), (1, y + 1 - 2 * (y % 2)), (3, 3 - y), (0, y)):
             send(pi.at[r, :, other, 1 - core], rc.at[r, :, other], base + C_RS + k, sib)
 
-    def scatter_users_start(r, own):
-        base = r * PER_ROUND + U_RS + 3 * own
-        place = slot if own else 1 - slot
-        send(pu.at[r, place, xo], um.at[r, own], base, xb_dev)
-        send(pu.at[r, place, x2], uz.at[r, own], base + 1, xb_dev)
-
     def scatter_items_y(r):
         base = r * PER_ROUND
 
         def halves(k, other):
             arrive(rc.at[r, :, other], base + C_RS + k, sib)
-            hb[r, other] = pi[r, :, other, core] + rc[r, :, other]
+            sums = pi[r, :, other, core] + rc[r, :, other]
+            hb[r, other] = sums.reshape(8, 16, 256)
 
         halves(2, yo)
-        send(hb.at[r, yo], ym.at[r], base + Y_RS, yb_dev)
+        for k in FAR_FIRST + (0,):
+            at = (z + k) % 8
+            send(hb.at[r, yo, at], ym.at[r, at], base + Y_RS + k, yb_dev)
         halves(1, y + 1 - 2 * (y % 2))
         halves(3, 3 - y)
-        send(hb.at[r, y2], yz.at[r], base + Y_RS + 1, yb_dev)
+        for k in FAR_FIRST + (0,):
+            at = (z + k) % 8
+            send(hb.at[r, y2, at], yz.at[r, at], base + Y_RS + 8 + k, yb_dev)
         halves(0, y)
 
-    def scatter_users_forward(r, own):
-        base = r * PER_ROUND + U_RS + 3 * own
-        place = slot if own else 1 - slot
-        arrive(um.at[r, own], base, xb_dev)
-        pu[r, place, x1] = pu[r, place, x1] + um[r, own]
-        send(pu.at[r, place, x1], ua.at[r, own], base + 2, xa_dev)
+    def scatter_items_forward(r):
+        base = r * PER_ROUND
+        for k in FAR_FIRST + (0,):
+            at = (z + k) % 8
+            arrive(ym.at[r, at], base + Y_RS + k, yb_dev)
+            hb[r, y1, at] = hb[r, y1, at] + ym[r, at]
+            send(hb.at[r, y1, at], ya.at[r, at], base + Y_RS + 16 + k, ya_dev)
 
     def scatter_items_z(r):
         base = r * PER_ROUND
-        arrive(ym.at[r], base + Y_RS, yb_dev)
-        hb[r, y1] = hb[r, y1] + ym[r]
-        send(hb.at[r, y1], ya.at[r], base + Y_RS + 2, ya_dev)
-        arrive(yz.at[r], base + Y_RS + 1, yb_dev)
-        arrive(ya.at[r], base + Y_RS + 2, ya_dev)
-        zs[r] = hb[r, y] + yz[r] + ya[r]
-        for k in range(1, 8):
-            dev, other_hi, other_lo = z_dev(k)
-            send(
-                zs.at[r, other_hi, pl.ds(pl.multiple_of(other_lo * 16, 16), 16)],
-                zb.at[r, k - 1],
-                base + Z_RS + k - 1,
-                dev,
-            )
-
-    def scatter_users_end(r, own):
-        base = r * PER_ROUND + U_RS + 3 * own
-        place = slot if own else 1 - slot
-        arrive(uz.at[r, own], base + 1, xb_dev)
-        arrive(ua.at[r, own], base + 2, xa_dev)
-        return pu[r, place, b] + uz[r, own] + ua[r, own]
-
-    def scatter_users_far(r):
-        pu[r, 1 - slot, b] = scatter_users_end(r, 0)
-        send(pu.at[r, 1 - slot, b], uq.at[r], r * PER_ROUND + U_RS + 6, far_dev)
-
-    def scatter_users_total(r):
-        total = scatter_users_end(r, 1)
-        if r:
-            arrive(uq.at[r], r * PER_ROUND + U_RS + 6, far_dev)
-            total = total + uq[r]
-        return total
-
-    def scatter_items_end(r):
-        base = r * PER_ROUND
-        total = zs[r, zhi, pl.ds(pl.multiple_of(c * 16, 16), 16)]
-        for k in range(1, 8):
+        for k in FAR_FIRST + (0,):
+            at = (z + k) % 8
+            arrive(yz.at[r, at], base + Y_RS + 8 + k, yb_dev)
+            arrive(ya.at[r, at], base + Y_RS + 16 + k, ya_dev)
+            zs[r, at] = hb[r, y, at] + yz[r, at] + ya[r, at]
+            if k:
+                send(zs.at[r, at], zb.at[r, k - 1], base + Z_RS + k - 1, z_dev(k)[0])
+
+    def scatter_items_total(r):
+        base = r * PER_ROUND
+        total = zs[r, z]
+        for k in NEAR_FIRST:
             arrive(zb.at[r, k - 1], base + Z_RS + k - 1, z_dev(8 - k)[0])
             total = total + zb[r, k - 1]
         return total
@@ -313,15 +373,38 @@
         scatter_items_y(r)
         scatter_users_forward(r, 1)
         if r:
-            scatter_users_far(r)
+            scatter_users_sum(r, 0)
+        scatter_items_forward(r)
         scatter_items_z(r)
         users = scatter_users_total(r)
-        items = scatter_items_end(r)
+        if r:
+            users = gu[...] + users
+        else:
+            gu[...] = users
+        if r < LAYERS:
+            gather_users_start(r + 1, users)
+        items = scatter_items_total(r)
+        if r:
+            items = gi[...] + items
+        else:
+            gi[...] = items
         return users, items
+
+    def send_tiles(first, last):
+        for n in range(first, last):
+            h = n // 3
+            start = (2 * h + 1 - c % 2) * GROUP + n % 3 * PIECE
+            send(
+                tiles_ref.at[pl.ds(start, PIECE)],
+                tbuf[h].at[1, pl.ds(n % 3 * PIECE, PIECE)],
+                TILES + n,
+                pair_dev,
+            )
 
     def place_tiles(h):
         own_tiles[h].wait()
-        arrive(tbuf[h].at[1, pl.ds(0, GROUP)], TILES + h, pair_dev)
+        for n in range(3 * h, 3 * h + 3):
+            arrive(tbuf[h].at[1, pl.ds(n % 3 * PIECE, PIECE)], TILES + n, pair_dev)
 
         def place(row, carry):
             at_row = pl.ds(pl.multiple_of(h * 512 + row * 128, 128), 128)
@@ -338,19 +421,17 @@
     to_scalars = pltpu.make_async_copy(gints, sints, lsem.at[2])
 
     def loss_gradient():
-        gather_start(0, uf_ref[...], if_ref[...])
         for k in range(1, 4):
             dev, other = hot_dev(k)
             send(gints.at[c], gints.at[c], INTS + k - 1, dev)
-        for h in range(2):
-            send(
-                tiles_ref.at[pl.ds((2 * h + 1 - c % 2) * GROUP, GROUP)],
-                tbuf[h].at[1, pl.ds(0, GROUP)],
-                TILES + h,
-                pair_dev,
-            )
+        gather_items_start(0, if_ref[...])
+        gather_users_start(0, uf_ref[...])
+        send_tiles(0, EARLY)
+        gather_items_z(0, NEAR_FIRST[:2])
         gather_users_forward(0, 1)
-        gather_items_z(0)
+        gather_items_forward(0, (0,))
+        gather_items_z(0, NEAR_FIRST[2:])
+        gather_items_forward(0, NEAR_FIRST[:2])
         for k in range(1, 4):
             dev, other = hot_dev(4 - k)
             arrive(gints.at[other], INTS + k - 1, dev)
@@ -360,19 +441,25 @@
             buyers = jnp.where(gints[h, 1:2, :] == c, gints[h, 0:1, :], -1)
             rows = lax.broadcasted_iota(jnp.int32, (512, 256), 0)
             ohu[:, span] = jnp.where(rows == buyers, 1.0, 0.0).astype(BF16)
+        gather_items_forward(0, NEAR_FIRST[2:])
+        for h in range(4):
+            span = slice(h * 256, (h + 1) * 256)
             rows = lax.broadcasted_iota(jnp.int32, (1024, 256), 0)
             chosen = jnp.where(rows == gints[h, 2:3, :], 1.0, 0.0)
             others = jnp.where(rows == gints[h, 3:4, :], 1.0, 0.0)
             ohd[:, span] = (chosen - others).astype(BF16)
-        gather_items_y(0)
+        gather_items_core(0)
         gather_users_end(0, 1)
         ut[0], ut[1], ut[2] = split3(ub[0, slot].reshape(512, 256).T)
+        for h in range(4):
+            span = slice(h * 256, (h + 1) * 256)
+            hot = ohu[:, span]
+            buy[:, span] = dot(ut[0], hot) + dot(ut[1], hot) + dot(ut[2], hot)
         gather_items_end(0)
         dt[0], dt[1], dt[2] = split3(ib[0].reshape(1024, 256).T)
         for h in range(4):
             span = slice(h * 256, (h + 1) * 256)
-            hot, signed = ohu[:, span], ohd[:, span]
-            buyer = dot(ut[0], hot) + dot(ut[1], hot) + dot(ut[2], hot)
+            buyer, signed = buy[:, span], ohd[:, span]
             differ = dot(dt[0], signed) + dot(dt[1], signed) + dot(dt[2], signed)
             margin = jnp.sum(buyer * differ, axis=0, keepdims=True)
             small = jnp.exp(-jnp.abs(margin))
@@ -388,18 +475,30 @@
         scatter_users_start(0, 1)
         return scatter(0)
 
-    def layer(r, users, items):
-        gather_start(r, users, items)
+    def layer(r, items):
+        gather_items_start(r, items)
         if r == 1:
+            send_tiles(EARLY, PIECES)
             to_scalars.wait()
             place_tiles(0)
+        gather_items_z(r, NEAR_FIRST[:2])
+        gather_users_forward(r, 1)
+        gather_items_forward(r, (0,))
+        gather_items_z(r, NEAR_FIRST[2:])
         gather_users_far(r)
-        gather_users_forward(r, 1)
-        gather_items_z(r)
+        gather_items_forward(r, NEAR_FIRST)
+        gather_items_core(r)
+        gather_users_forward(r, 0)
+        gather_items_end(r)
         if r == 1:
             place_tiles(1)
-        gather_users_forward(r, 0)
-        gather_items_y(r)
+        xh, xl = split2(ib[r].reshape(1024, 256))
+        for own in range(2):
+            place = place_of(own)
+            rows = pl.ds(pl.multiple_of(place * 512, 512), 512)
+            sums = dot(ah[rows], xh) + dot(ah[rows], xl) + dot(al[rows], xh)
+            pu[r, place] = sums.reshape(4, 128, 256)
+            scatter_users_start(r, own)
         gather_users_end(r, 1)
         gather_users_end(r, 0)
         uh, ul = split2(ub[r].reshape(1024, 256))
@@ -407,23 +506,12 @@
             rows = slice(m * 256, (m + 1) * 256)
             store_items(r, m, dot(ath[rows], uh) + dot(ath[rows], ul) + dot(atl[rows], uh))
         scatter_items_core(r)
-        gather_items_end(r)
-        xh, xl = split2(ib[r].reshape(1024, 256))
-        for own in range(2):
-            place = slot if own else 1 - slot
-            rows = pl.ds(pl.multiple_of(place * 512, 512), 512)
-            sums = dot(ah[rows], xh) + dot(ah[rows], xl) + dot(al[rows], xh)
-            pu[r, place] = sums.reshape(4, 128, 256)
-            scatter_users_start(r, own)
-        users, items = scatter(r)
-        return gu[...] + users, gi[...] + items
+        return scatter(r)
 
     def rounds():
         users, items = loss_gradient()
-        gu[...] = users
-        gi[...] = items
         for r in range(1, ROUNDS):
-            users, items = layer(r, users, items)
+            users, items = layer(r, items)
         return users, items
 
     users, items = rounds()
@@ -477,12 +565,13 @@
             pltpu.VMEM((1024, 1024), BF16),
             pltpu.VMEM((512, 1024), BF16),
             pltpu.VMEM((1024, 1024), BF16),
+            pltpu.VMEM((256, 1024), F32),
             pltpu.VMEM((3, 256, 512), BF16),
             pltpu.VMEM((3, 256, 1024), BF16),
             pltpu.VMEM((2, 256, 1024), BF16),
             pltpu.VMEM((2, 256, 1024), BF16),
             pltpu.VMEM((ROUNDS, 2, 4, 128, 256), F32),
-            pltpu.VMEM((ROUNDS, 2, 4, 2, 64, 256), F32),
+            pltpu.VMEM((ROUNDS, 2, 4, 2, 4, 16, 256), F32),
             pltpu.VMEM((ROUNDS, 2, 4, 128, 256), F32),
             pltpu.VMEM((ROUNDS, 2, 4, 2, 64, 256), F32),
             pltpu.VMEM((ROUNDS, 2, 128, 256), F32),
@@ -490,11 +579,11 @@
             pltpu.VMEM((ROUNDS, 2, 128, 256), F32),
             pltpu.VMEM((ROUNDS, 128, 256), F32),
             pltpu.VMEM((ROUNDS, 2, 4, 64, 256), F32),
-            pltpu.VMEM((ROUNDS, 4, 2, 64, 256), F32),
-            pltpu.VMEM((ROUNDS, 2, 64, 256), F32),
-            pltpu.VMEM((ROUNDS, 2, 64, 256), F32),
-            pltpu.VMEM((ROUNDS, 2, 64, 256), F32),
-            pltpu.VMEM((ROUNDS, 2, 64, 256), F32),
+            pltpu.VMEM((ROUNDS, 4, 8, 16, 256), F32),
+            pltpu.VMEM((ROUNDS, 8, 16, 256), F32),
+            pltpu.VMEM((ROUNDS, 8, 16, 256), F32),
+            pltpu.VMEM((ROUNDS, 8, 16, 256), F32),
+            pltpu.VMEM((ROUNDS, 8, 16, 256), F32),
             pltpu.VMEM((ROUNDS, 7, 16, 256), F32),
             pltpu.VMEM((128, 256), F32),
             pltpu.VMEM((16, 256), F32),

time: 143 us -> 129 us (0.902)
  Pallas kernels: 136 us -> 123 us
    pallas_call x1, Pallas kernels: 136 us -> 123 us  [body(): pl.pallas_call(kernel, out_shape=(jax.ShapeDtypeStruct((128, 256), F32),...]
where the time goes in v3:
time: 129 us
  Pallas kernels  123 us (95%)
  local copies, waits for them, and re-layouts  2.91 us (2%)
  other arithmetic  1.64 us (1%)
  between operations  1.33 us (1%)
    pallas_call x1, Pallas kernels, body(): pl.pallas_call(kernel, out_shape=(jax.ShapeDtypeStruct((128, 256), F32),...  123 us
    unnamed x6, local copies, waits for them, and re-layouts  2.88 us

profile of v3, /device:TPU:1, one launch (start us, length us, event | category | flops | bytes accessed | tf_op | source)
XLA Modules:
  0.0 129.2 jit_solution(11801849165927112313)
XLA Ops:
  1.3 0.7 compare_select_fusion.4
  2.0 0.1 select_reduce_fusion
  2.1 0.8 and_select_fusion.4
  3.0 0.0 copy-start
  3.0 0.9 copy-done
  3.9 0.0 copy-start.1
  3.9 0.7 copy-done.1
  4.6 123.3 %propagate.1 = (f32[128,256]{1,0:T(8,128)S(1)}, f32[16,256]{1,0:T(8,128)S(1)}) custom-call(s32[8,256]{1,0:T(8,128)S(1)} %stack.15.ints_ref, f32[128,256]{1,0:T(8,128)S(1)} %copy-done, f32[16,256]{1,0:T(8,128)S(1)} %copy-done.1, f32[48,128,128]{2,1,0:T(8,128)} %tiles_ref.1), custom_call_target="tpu_custom_call" | custom-call | tf_op jit(solution)/shard_map/propagate/pallas_call | solution.py:549
  128.0 0.7 copy.12
  128.6 0.6 copy.13
  (6 shorter events, 0.1 us)
Async XLA Ops:
  3.0 0.9 copy-start
  3.9 0.7 copy-start.1

commit v4 on v3

--- a/solution.py
+++ b/solution.py
@@ -25,7 +25,7 @@
 Z_AG = U_AG + 7 * CHUNKS
 Y_AG = Z_AG + 7
 C_AG = Y_AG + 24
-C_RS = C_AG + 11
+C_RS = C_AG + 32
 Y_RS = C_RS + 4
 Z_RS = Y_RS + 24
 U_RS = Z_RS + 7
@@ -119,12 +119,11 @@
         return first, second, (v + 2) % 4
 
     x1, x2, xo = ring(b)
-    y1, y2, yo = ring(y)
-    ya_dev = (user_index(zhi, y1, core), b, c)
-    yb_dev = (user_index(zhi, y2, core), b, c)
     xa_dev = (a, x1, c)
     xb_dev = (a, x2, c)
+    xo_dev = (a, xo, c)
     tbuf = (tbuf0, tbuf1)
+    yb = (ym, ya, yz)
     slot = c // 2
     pair = c + 1 - 2 * (c % 2)
     pair_dev = (a, b, pair)
@@ -134,6 +133,10 @@
     def z_dev(k):
         other = (z + k) % 8
         return (user_index(other // 4, y, core), b, other % 4), other // 4, other % 4
+
+    def y_dev(k):
+        other = (y + k) % 4
+        return (user_index(zhi, other, core), b, c)
 
     def hot_dev(k):
         other = (c + k) % 4
@@ -164,7 +167,8 @@
         ).wait_recv()
 
     barrier = pltpu.get_barrier_semaphore()
-    peers = [xa_dev, xb_dev, ya_dev, yb_dev, sib] + [z_dev(k)[0] for k in range(1, 8)]
+    peers = [xa_dev, xb_dev, xo_dev, sib]
+    peers += [y_dev(k) for k in range(1, 4)] + [z_dev(k)[0] for k in range(1, 8)]
     for dev in peers:
         pl.semaphore_signal(barrier, inc=1, device_id=dev, device_id_type=MESH)
     own_tiles = [
@@ -198,32 +202,42 @@
         ub[r, slot, b] = users
         for q in range(CHUNKS):
             mine = ub.at[r, slot, b, chunk(q)]
-            if r:
-                send(mine, mine, base + 6 * CHUNKS + q, far_dev)
             send(mine, mine, base + q, xa_dev)
             send(mine, mine, base + CHUNKS + q, xb_dev)
 
-    def gather_users_far(r):
+    def gather_users_over_z(r):
+        for q in range(CHUNKS):
+            mine = ub.at[r, slot, b, chunk(q)]
+            send(mine, mine, r * PER_ROUND + U_AG + 6 * CHUNKS + q, far_dev)
+
+    def gather_users_far(r, chunks):
         base = r * PER_ROUND + U_AG
-        for q in range(CHUNKS):
+        for q in chunks:
             other = ub.at[r, 1 - slot, b, chunk(q)]
             arrive(other, base + 6 * CHUNKS + q, far_dev)
+            send(other, other, base + 5 * CHUNKS + q, xo_dev)
             send(other, other, base + 3 * CHUNKS + q, xa_dev)
             send(other, other, base + 4 * CHUNKS + q, xb_dev)
 
-    def gather_users_forward(r, own):
-        base = r * PER_ROUND + U_AG + (0 if own else 3 * CHUNKS)
-        for q in range(CHUNKS):
-            block = ub.at[r, place_of(own), x1, chunk(q)]
+    def gather_users_forward(r):
+        base = r * PER_ROUND + U_AG
+        for q in range(CHUNKS):
+            block = ub.at[r, slot, x1, chunk(q)]
             arrive(block, base + q, xa_dev)
             send(block, block, base + 2 * CHUNKS + q, xb_dev)
 
-    def gather_users_end(r, own):
-        base = r * PER_ROUND + U_AG + (0 if own else 3 * CHUNKS)
-        for q in range(CHUNKS):
-            arrive(ub.at[r, place_of(own), x2, chunk(q)], base + CHUNKS + q, xb_dev)
-        for q in range(CHUNKS):
-            arrive(ub.at[r, place_of(own), xo, chunk(q)], base + 2 * CHUNKS + q, xb_dev)
+    def gather_users_end(r):
+        base = r * PER_ROUND + U_AG
+        for q in range(CHUNKS):
+            arrive(ub.at[r, slot, x2, chunk(q)], base + CHUNKS + q, xb_dev)
+        for q in range(CHUNKS):
+            arrive(ub.at[r, slot, xo, chunk(q)], base + 2 * CHUNKS + q, xb_dev)
+        if r:
+            base = base + 3 * CHUNKS
+            for q in range(CHUNKS):
+                arrive(ub.at[r, 1 - slot, x1, chunk(q)], base + q, xa_dev)
+                arrive(ub.at[r, 1 - slot, x2, chunk(q)], base + CHUNKS + q, xb_dev)
+                arrive(ub.at[r, 1 - slot, xo, chunk(q)], base + 2 * CHUNKS + q, xo_dev)
 
     def scatter_users_start(r, own):
         base = r * PER_ROUND + U_RS + 3 * CHUNKS * own
@@ -269,89 +283,68 @@
         mine = ib.at[r, zhi, y, core, c]
         for k in FAR_FIRST:
             send(mine, mine, base + Z_AG + k - 1, z_dev(k)[0])
-        send(mine, mine, base + Y_AG, ya_dev)
-        send(mine, mine, base + Y_AG + 8, yb_dev)
+        pass_on(r, 0)
+
+    def pass_on(r, k):
+        base = r * PER_ROUND
+        hi, lo = along_z(k)
+        piece = ib.at[r, hi, y, core, lo]
+        for d in (2, 1, 3):
+            send(piece, piece, base + Y_AG + (d - 1) * 8 + k, y_dev(d))
+        send(piece, piece, base + C_AG + k, sib)
 
     def gather_items_z(r, steps):
         base = r * PER_ROUND
         for k in steps:
             hi, lo = along_z(k)
-            piece = ib.at[r, hi, y, core, lo]
-            arrive(piece, base + Z_AG + (8 - k) - 1, z_dev(k)[0])
-            send(piece, piece, base + Y_AG + k, ya_dev)
-            send(piece, piece, base + Y_AG + 8 + k, yb_dev)
-
-    def gather_items_forward(r, steps):
+            arrive(ib.at[r, hi, y, core, lo], base + Z_AG + (8 - k) - 1, z_dev(k)[0])
+            pass_on(r, k)
+
+    def gather_items_y(r, steps):
         base = r * PER_ROUND
         for k in steps:
             hi, lo = along_z(k)
-            piece = ib.at[r, hi, y1, core, lo]
-            arrive(piece, base + Y_AG + k, ya_dev)
-            send(piece, piece, base + Y_AG + 16 + k, yb_dev)
-
-    def gather_items_core(r):
-        base = r * PER_ROUND
-        for index, other in ((0, y), (1 + core, y1)):
-            block = ib.at[r, :, other, core]
-            send(block, block, base + C_AG + index, sib)
+            for d in (1, 3, 2):
+                piece = ib.at[r, hi, (y + d) % 4, core, lo]
+                arrive(piece, base + Y_AG + (3 - d) * 8 + k, y_dev(d))
+                send(piece, piece, base + C_AG + d * 8 + k, sib)
+
+    def gather_items_end(r):
+        base = r * PER_ROUND
         for k in (0,) + NEAR_FIRST:
             hi, lo = along_z(k)
-            arrive(ib.at[r, hi, y2, core, lo], base + Y_AG + 8 + k, yb_dev)
-        block = ib.at[r, :, y2, core]
-        send(block, block, base + C_AG + 2 - core, sib)
-        for k in (0,) + NEAR_FIRST:
-            hi, lo = along_z(k)
-            piece = ib.at[r, hi, yo, core, lo]
-            arrive(piece, base + Y_AG + 16 + k, yb_dev)
-            send(piece, piece, base + C_AG + 3 + k, sib)
-
-    def gather_items_end(r):
-        base = r * PER_ROUND
-        for index, other in ((0, y), (1, y + 1 - 2 * (y % 2)), (2, 3 - y)):
-            arrive(ib.at[r, :, other, 1 - core], base + C_AG + index, sib)
-        for k in (0,) + NEAR_FIRST:
-            hi, lo = along_z(k)
-            arrive(ib.at[r, hi, yo, 1 - core, lo], base + C_AG + 3 + k, sib)
+            for d in range(4):
+                piece = ib.at[r, hi, (y + d) % 4, 1 - core, lo]
+                arrive(piece, base + C_AG + d * 8 + k, sib)
 
     def scatter_items_core(r):
         base = r * PER_ROUND
-        for k, other in ((2, yo), (1, y + 1 - 2 * (y % 2)), (3, 3 - y), (0, y)):
-            send(pi.at[r, :, other, 1 - core], rc.at[r, :, other], base + C_RS + k, sib)
+        for d in (2, 1, 3, 0):
+            other = (y + d) % 4
+            send(pi.at[r, :, other, 1 - core], rc.at[r, :, other], base + C_RS + d, sib)
 
     def scatter_items_y(r):
         base = r * PER_ROUND
-
-        def halves(k, other):
-            arrive(rc.at[r, :, other], base + C_RS + k, sib)
+        for d in (2, 1, 3, 0):
+            other = (y + d) % 4
+            arrive(rc.at[r, :, other], base + C_RS + d, sib)
             sums = pi[r, :, other, core] + rc[r, :, other]
             hb[r, other] = sums.reshape(8, 16, 256)
-
-        halves(2, yo)
         for k in FAR_FIRST + (0,):
             at = (z + k) % 8
-            send(hb.at[r, yo, at], ym.at[r, at], base + Y_RS + k, yb_dev)
-        halves(1, y + 1 - 2 * (y % 2))
-        halves(3, 3 - y)
-        for k in FAR_FIRST + (0,):
+            for d in (2, 1, 3):
+                source = hb.at[r, (y + d) % 4, at]
+                send(source, yb[d - 1].at[r, at], base + Y_RS + (d - 1) * 8 + k, y_dev(d))
+
+    def scatter_items_z(r, steps):
+        base = r * PER_ROUND
+        for k in steps:
             at = (z + k) % 8
-            send(hb.at[r, y2, at], yz.at[r, at], base + Y_RS + 8 + k, yb_dev)
-        halves(0, y)
-
-    def scatter_items_forward(r):
-        base = r * PER_ROUND
-        for k in FAR_FIRST + (0,):
-            at = (z + k) % 8
-            arrive(ym.at[r, at], base + Y_RS + k, yb_dev)
-            hb[r, y1, at] = hb[r, y1, at] + ym[r, at]
-            send(hb.at[r, y1, at], ya.at[r, at], base + Y_RS + 16 + k, ya_dev)
-
-    def scatter_items_z(r):
-        base = r * PER_ROUND
-        for k in FAR_FIRST + (0,):
-            at = (z + k) % 8
-            arrive(yz.at[r, at], base + Y_RS + 8 + k, yb_dev)
-            arrive(ya.at[r, at], base + Y_RS + 16 + k, ya_dev)
-            zs[r, at] = hb[r, y, at] + yz[r, at] + ya[r, at]
+            total = hb[r, y, at]
+            for d in range(1, 4):
+                arrive(yb[d - 1].at[r, at], base + Y_RS + (d - 1) * 8 + k, y_dev(d))
+                total = total + yb[d - 1][r, at]
+            zs[r, at] = total
             if k:
                 send(zs.at[r, at], zb.at[r, k - 1], base + Z_RS + k - 1, z_dev(k)[0])
 
@@ -372,10 +365,10 @@
             scatter_users_forward(r, 0)
         scatter_items_y(r)
         scatter_users_forward(r, 1)
+        scatter_items_z(r, FAR_FIRST[:3])
         if r:
             scatter_users_sum(r, 0)
-        scatter_items_forward(r)
-        scatter_items_z(r)
+        scatter_items_z(r, FAR_FIRST[3:] + (0,))
         users = scatter_users_total(r)
         if r:
             users = gu[...] + users
@@ -428,10 +421,7 @@
         gather_users_start(0, uf_ref[...])
         send_tiles(0, EARLY)
         gather_items_z(0, NEAR_FIRST[:2])
-        gather_users_forward(0, 1)
-        gather_items_forward(0, (0,))
-        gather_items_z(0, NEAR_FIRST[2:])
-        gather_items_forward(0, NEAR_FIRST[:2])
+        gather_users_forward(0)
         for k in range(1, 4):
             dev, other = hot_dev(4 - k)
             arrive(gints.at[other], INTS + k - 1, dev)
@@ -441,15 +431,15 @@
             buyers = jnp.where(gints[h, 1:2, :] == c, gints[h, 0:1, :], -1)
             rows = lax.broadcasted_iota(jnp.int32, (512, 256), 0)
             ohu[:, span] = jnp.where(rows == buyers, 1.0, 0.0).astype(BF16)
-        gather_items_forward(0, NEAR_FIRST[2:])
+        gather_items_z(0, NEAR_FIRST[2:])
         for h in range(4):
             span = slice(h * 256, (h + 1) * 256)
             rows = lax.broadcasted_iota(jnp.int32, (1024, 256), 0)
             chosen = jnp.where(rows == gints[h, 2:3, :], 1.0, 0.0)
             others = jnp.where(rows == gints[h, 3:4, :], 1.0, 0.0)
             ohd[:, span] = (chosen - others).astype(BF16)
-        gather_items_core(0)
-        gather_users_end(0, 1)
+        gather_items_y(0, (0,) + NEAR_FIRST)
+        gather_users_end(0)
         ut[0], ut[1], ut[2] = split3(ub[0, slot].reshape(512, 256).T)
         for h in range(4):
             span = slice(h * 256, (h + 1) * 256)
@@ -477,18 +467,19 @@
 
     def layer(r, items):
         gather_items_start(r, items)
+        gather_users_over_z(r)
         if r == 1:
             send_tiles(EARLY, PIECES)
             to_scalars.wait()
             place_tiles(0)
         gather_items_z(r, NEAR_FIRST[:2])
-        gather_users_forward(r, 1)
-        gather_items_forward(r, (0,))
-        gather_items_z(r, NEAR_FIRST[2:])
-        gather_users_far(r)
-        gather_items_forward(r, NEAR_FIRST)
-        gather_items_core(r)
-        gather_users_forward(r, 0)
+        gather_users_forward(r)
+        gather_items_z(r, NEAR_FIRST[2:6])
+        gather_users_far(r, (0, 1))
+        gather_items_z(r, NEAR_FIRST[6:])
+        gather_items_y(r, (0,) + NEAR_FIRST[:4])
+        gather_users_far(r, (2, 3))
+        gather_items_y(r, NEAR_FIRST[4:])
         gather_items_end(r)
         if r == 1:
             place_tiles(1)
@@ -499,8 +490,7 @@
             sums = dot(ah[rows], xh) + dot(ah[rows], xl) + dot(al[rows], xh)
             pu[r, place] = sums.reshape(4, 128, 256)
             scatter_users_start(r, own)
-        gather_users_end(r, 1)
-        gather_users_end(r, 0)
+        gather_users_end(r)
         uh, ul = split2(ub[r].reshape(1024, 256))
         for m in range(4):
             rows = slice(m * 256, (m + 1) * 256)

time: 129 us -> 130 us (level)
  no operation moved by 1% of the time
where the time goes in v4:
time: 130 us
  Pallas kernels  124 us (95%)
  local copies, waits for them, and re-layouts  2.91 us (2%)
  other arithmetic  1.64 us (1%)
  between operations  1.33 us (1%)
    pallas_call x1, Pallas kernels, body(): pl.pallas_call(kernel, out_shape=(jax.ShapeDtypeStruct((128, 256), F32),...  124 us
    unnamed x6, local copies, waits for them, and re-layouts  2.88 us

profile of v4, /device:TPU:1, one launch (start us, length us, event | category | flops | bytes accessed | tf_op | source)
XLA Modules:
  0.0 129.8 jit_solution(3709394777746560409)
XLA Ops:
  1.3 0.7 compare_select_fusion.4
  2.0 0.1 select_reduce_fusion
  2.1 0.8 and_select_fusion.4
  3.0 0.0 copy-start
  3.0 0.9 copy-done
  3.9 0.0 copy-start.1
  3.9 0.7 copy-done.1
  4.6 123.9 %propagate.1 = (f32[128,256]{1,0:T(8,128)S(1)}, f32[16,256]{1,0:T(8,128)S(1)}) custom-call(s32[8,256]{1,0:T(8,128)S(1)} %stack.15.ints_ref, f32[128,256]{1,0:T(8,128)S(1)} %copy-done, f32[16,256]{1,0:T(8,128)S(1)} %copy-done.1, f32[48,128,128]{2,1,0:T(8,128)} %tiles_ref.1), custom_call_target="tpu_custom_call" | custom-call | tf_op jit(solution)/shard_map/propagate/pallas_call | solution.py:539
  128.5 0.7 copy.12
  129.2 0.6 copy.13
  (6 shorter events, 0.1 us)
Async XLA Ops:
  3.0 0.9 copy-start
  3.9 0.7 copy-start.1

commit v5 on v4

--- a/solution.py
+++ b/solution.py
@@ -58,12 +58,16 @@
 
 
 def kernel(
-    ints_ref,
+    trip_ref,
+    rows_ref,
+    cols_ref,
+    count_ref,
     uf_ref,
     if_ref,
     tiles_ref,
     uo_ref,
     io_ref,
+    trips,
     gints,
     sints,
     tbuf0,
@@ -126,6 +130,7 @@
     yb = (ym, ya, yz)
     slot = c // 2
     pair = c + 1 - 2 * (c % 2)
+    from_pair = 3 - 2 * (c % 2)
     pair_dev = (a, b, pair)
     far_dev = (a, b, (c + 2) % 4)
     sib = (user_index(zhi, y, 1 - core), b, c)
@@ -181,10 +186,52 @@
     ]
     for copy in own_tiles:
         copy.start()
+    shares = [
+        pltpu.make_async_copy(trip_ref, trips, lsem.at[3]),
+        pltpu.make_async_copy(uf_ref, ub.at[0, slot, b], lsem.at[4]),
+        pltpu.make_async_copy(if_ref, ib.at[0, zhi, y, core, c], lsem.at[5]),
+    ]
+    for copy in shares:
+        copy.start()
     for h in range(2):
         tbuf[h][0, GROUP] = jnp.zeros((128, 128), F32)
         tbuf[h][1, GROUP] = jnp.zeros((128, 128), F32)
-    gints[c] = ints_ref[...]
+    for copy in shares:
+        copy.wait()
+    lanes = lax.broadcasted_iota(jnp.int32, (1, 128), 1)
+    source = jnp.full((1, 128), GROUP, jnp.int32)
+    for n in range(4 * GROUP):
+        spot = n // GROUP * PLACES + rows_ref[n] // 4 * 8 + cols_ref[n]
+        spot = jnp.where(n < count_ref[0], spot, -1)
+        source = jnp.where(lanes == spot, n % GROUP, source)
+    own = trips[...].T
+    buyers = own[0:1] % 2048
+    gints[0, 0:1] = buyers // 512 * 128 + buyers % 128
+    gints[0, 1:2] = buyers // 128 % 4
+    gints[0, 2:3] = own[1:2] // 256 * 64 + own[1:2] % 64
+    gints[0, 3:4] = own[2:3] // 256 * 64 + own[2:3] % 64
+    gints[0, 4:5, 0:128] = source
+    gints[0, 4:5, 128:256] = source
+    gints[0, 5:8] = jnp.zeros((3, 256), jnp.int32)
+    count_up = lax.broadcasted_iota(jnp.int32, (256, 256), 0).astype(F32).astype(BF16)
+
+    def one_hot(index, m):
+        inside = jnp.where(index // 256 == m, index % 256, -1).astype(F32)
+        inside = jnp.broadcast_to(inside, (256, 256)).astype(BF16)
+        return jnp.where(count_up == inside, jnp.ones((), BF16), jnp.zeros((), BF16))
+
+    def select_users(k):
+        buyers = jnp.where(gints[k, 1:2, :] == c, gints[k, 0:1, :], -1)
+        for m in range(2):
+            ohu[m * 256 : (m + 1) * 256, k * 256 : (k + 1) * 256] = one_hot(buyers, m)
+
+    def select_items(k):
+        for m in range(4):
+            signed = one_hot(gints[k, 2:3, :], m) - one_hot(gints[k, 3:4, :], m)
+            ohd[m * 256 : (m + 1) * 256, k * 256 : (k + 1) * 256] = signed
+
+    select_users(0)
+    select_items(0)
     pl.semaphore_wait(barrier, len(peers))
 
     def chunk(q):
@@ -199,7 +246,8 @@
 
     def gather_users_start(r, users):
         base = r * PER_ROUND + U_AG
-        ub[r, slot, b] = users
+        if r:
+            ub[r, slot, b] = users
         for q in range(CHUNKS):
             mine = ub.at[r, slot, b, chunk(q)]
             send(mine, mine, base + q, xa_dev)
@@ -279,7 +327,8 @@
 
     def gather_items_start(r, items):
         base = r * PER_ROUND
-        ib[r, zhi, y, core, c] = items
+        if r:
+            ib[r, zhi, y, core, c] = items
         mine = ib.at[r, zhi, y, core, c]
         for k in FAR_FIRST:
             send(mine, mine, base + Z_AG + k - 1, z_dev(k)[0])
@@ -365,10 +414,15 @@
             scatter_users_forward(r, 0)
         scatter_items_y(r)
         scatter_users_forward(r, 1)
+        if r == 0:
+            to_scalars.wait()
+            place_tiles(0)
         scatter_items_z(r, FAR_FIRST[:3])
         if r:
             scatter_users_sum(r, 0)
         scatter_items_z(r, FAR_FIRST[3:] + (0,))
+        if r == 0:
+            send_tiles(EARLY, EARLY + 1)
         users = scatter_users_total(r)
         if r:
             users = gu[...] + users
@@ -404,7 +458,7 @@
             for col in range(8):
                 at_col = slice(col * 128, (col + 1) * 128)
                 spot = (2 * h + c % 2) * PLACES + row * 8 + col
-                tile = tbuf[h][0, sints[c, 4, spot]] + tbuf[h][1, sints[pair, 4, spot]]
+                tile = tbuf[h][0, sints[0, 4, spot]] + tbuf[h][1, sints[from_pair, 4, spot]]
                 ah[at_row, at_col], al[at_row, at_col] = split2(tile)
                 ath[at_col, at_row], atl[at_col, at_row] = split2(tile.T)
             return carry
@@ -416,29 +470,22 @@
     def loss_gradient():
         for k in range(1, 4):
             dev, other = hot_dev(k)
-            send(gints.at[c], gints.at[c], INTS + k - 1, dev)
-        gather_items_start(0, if_ref[...])
-        gather_users_start(0, uf_ref[...])
+            send(gints.at[0], gints.at[k], INTS + k - 1, dev)
+        gather_items_start(0, None)
+        gather_users_start(0, None)
         send_tiles(0, EARLY)
         gather_items_z(0, NEAR_FIRST[:2])
         gather_users_forward(0)
         for k in range(1, 4):
-            dev, other = hot_dev(4 - k)
-            arrive(gints.at[other], INTS + k - 1, dev)
+            arrive(gints.at[k], INTS + k - 1, hot_dev(4 - k)[0])
         to_scalars.start()
-        for h in range(4):
-            span = slice(h * 256, (h + 1) * 256)
-            buyers = jnp.where(gints[h, 1:2, :] == c, gints[h, 0:1, :], -1)
-            rows = lax.broadcasted_iota(jnp.int32, (512, 256), 0)
-            ohu[:, span] = jnp.where(rows == buyers, 1.0, 0.0).astype(BF16)
         gather_items_z(0, NEAR_FIRST[2:])
-        for h in range(4):
-            span = slice(h * 256, (h + 1) * 256)
-            rows = lax.broadcasted_iota(jnp.int32, (1024, 256), 0)
-            chosen = jnp.where(rows == gints[h, 2:3, :], 1.0, 0.0)
-            others = jnp.where(rows == gints[h, 3:4, :], 1.0, 0.0)
-            ohd[:, span] = (chosen - others).astype(BF16)
-        gather_items_y(0, (0,) + NEAR_FIRST)
+        for k in range(1, 4):
+            select_users(k)
+        gather_items_y(0, (0,) + NEAR_FIRST[:4])
+        for k in range(1, 4):
+            select_items(k)
+        gather_items_y(0, NEAR_FIRST[4:])
         gather_users_end(0)
         ut[0], ut[1], ut[2] = split3(ub[0, slot].reshape(512, 256).T)
         for h in range(4):
@@ -469,9 +516,7 @@
         gather_items_start(r, items)
         gather_users_over_z(r)
         if r == 1:
-            send_tiles(EARLY, PIECES)
-            to_scalars.wait()
-            place_tiles(0)
+            send_tiles(EARLY + 1, PIECES)
         gather_items_z(r, NEAR_FIRST[:2])
         gather_users_forward(r)
         gather_items_z(r, NEAR_FIRST[2:6])
@@ -512,39 +557,19 @@
 
 
 def body(user_final, item_final, tiles, tile_rows, tile_cols, tile_count, triplets):
-    slots = tiles.shape[0]
-    buyers = triplets[:, 0] % 2048
-    chosen = triplets[:, 1] // 256 * 64 + triplets[:, 1] % 64
-    others = triplets[:, 2] // 256 * 64 + triplets[:, 2] % 64
-    slot = jnp.arange(slots, dtype=jnp.int32)
-    spot = slot // GROUP * PLACES + tile_rows // 4 * 8 + tile_cols
-    spot = jnp.where(slot < tile_count[0], spot, -1)
-    match = spot[None, :] == jnp.arange(4 * PLACES, dtype=jnp.int32)[:, None]
-    source = GROUP + jnp.sum(jnp.where(match, slot % GROUP - GROUP, 0), axis=1)
-    source = jnp.concatenate([source, source])
-    blank = jnp.zeros_like(source)
-    ints = jnp.stack(
-        [
-            buyers // 512 * 128 + buyers % 128,
-            buyers // 128 % 4,
-            chosen,
-            others,
-            source,
-            blank,
-            blank,
-            blank,
-        ]
-    ).astype(jnp.int32)
     vmem = pl.BlockSpec(memory_space=pltpu.VMEM)
+    smem = pl.BlockSpec(memory_space=pltpu.SMEM)
+    anywhere = pl.BlockSpec(memory_space=pl.ANY)
     return pl.pallas_call(
         kernel,
         out_shape=(
             jax.ShapeDtypeStruct((128, 256), F32),
             jax.ShapeDtypeStruct((16, 256), F32),
         ),
-        in_specs=[vmem, vmem, vmem, pl.BlockSpec(memory_space=pl.ANY)],
+        in_specs=[anywhere, smem, smem, smem, anywhere, anywhere, anywhere],
         out_specs=(vmem, vmem),
         scratch_shapes=[
+            pltpu.VMEM((256, 3), jnp.int32),
             pltpu.VMEM((4, 8, 256), jnp.int32),
             pltpu.SMEM((4, 8, 256), jnp.int32),
             pltpu.VMEM((2, GROUP + 1, 128, 128), F32),
@@ -579,13 +604,13 @@
             pltpu.VMEM((16, 256), F32),
             pltpu.SemaphoreType.DMA((COPIES,)),
             pltpu.SemaphoreType.DMA((COPIES,)),
-            pltpu.SemaphoreType.DMA((3,)),
+            pltpu.SemaphoreType.DMA((6,)),
         ],
         compiler_params=pltpu.CompilerParams(
             collective_id=0, has_side_effects=True, vmem_limit_bytes=52 * 1024 * 1024
         ),
         name="propagate",
-    )(ints, user_final, item_final, tiles)
+    )(triplets, tile_rows, tile_cols, tile_count, user_final, item_final, tiles)
 
 
 def solution(mesh):

time: 130 us -> 130 us (level)
  local copies, waits for them, and re-layouts: 2.91 us -> 5.01 us
  other arithmetic: 1.64 us -> 0 us
    unnamed x6 -> x11, local copies, waits for them, and re-layouts: 2.88 us -> 5.01 us
    select_n x2 -> x0, other arithmetic: 1.52 us -> none  [the longest x1 0.83 us: body(): buyers // 128 % 4]
where the time goes in v5:
time: 130 us
  Pallas kernels  124 us (95%)
  local copies, waits for them, and re-layouts  5.01 us (4%)
  between operations  1.3 us (1%)
    pallas_call x1, Pallas kernels, body(): pl.pallas_call(kernel, out_shape=(jax.ShapeDtypeStruct((128, 256), F32),...  124 us
    unnamed x11, local copies, waits for them, and re-layouts  5.01 us

profile of v5, /device:TPU:1, one launch (start us, length us, event | category | flops | bytes accessed | tf_op | source)
XLA Modules:
  0.0 130.2 jit_solution(11716511145899531379)
XLA Ops:
  1.3 0.8 copy.9.trip_ref
  2.1 0.0 copy-start
  2.1 0.9 copy-done
  3.0 0.0 copy-start.1
  3.0 0.7 copy-done.1
  3.7 0.0 copy-start.2
  3.7 0.7 copy-done.2
  4.4 0.0 copy-start.3
  4.4 0.7 copy-done.3
  5.0 123.9 %propagate.1 = (f32[128,256]{1,0:T(8,128)S(1)}, f32[16,256]{1,0:T(8,128)S(1)}) custom-call(s32[256,3]{1,0:T(8,128)S(1)} %copy.9.trip_ref, s32[48]{0:T(128)S(1)} %copy-done.2, s32[48]{0:T(128)S(1)} %copy-done.3, s32[1]{0:T(128)S(6)} %copy.12.count_ref, f32[128,256]{1,0:T(8,128)S(1)} %copy-done, f32[16,256]{1,0:T(8,128)S(1)} %copy-done.1, ...), custom_call_target="tpu_custom_call" | custom-call | tf_op jit(solution)/shard_map/propagate/pallas_call | solution.py:563
  128.9 0.7 copy.13
  129.6 0.6 copy.14
Async XLA Ops:
  2.1 0.9 copy-start
  3.0 0.7 copy-start.1
  3.7 0.7 copy-start.2
  4.4 0.7 copy-start.3

commit v6 on v5

--- a/solution.py
+++ b/solution.py
@@ -31,7 +31,8 @@
 U_RS = Z_RS + 7
 PER_ROUND = U_RS + 7 * CHUNKS
 INTS = PER_ROUND * ROUNDS
-TILES = INTS + 3
+SOURCE = INTS + 3
+TILES = SOURCE + 1
 COPIES = TILES + PIECES
 NEAR_FIRST = (1, 7, 2, 6, 3, 5, 4)
 FAR_FIRST = (4, 5, 3, 6, 2, 7, 1)
@@ -53,22 +54,16 @@
     return jnp.dot(a, b, preferred_element_type=F32)
 
 
-def dot_nt(a, b):
-    return lax.dot_general(a, b, (((1,), (1,)), ((), ())), preferred_element_type=F32)
-
-
 def kernel(
     trip_ref,
-    rows_ref,
-    cols_ref,
-    count_ref,
+    spot_ref,
     uf_ref,
     if_ref,
     tiles_ref,
     uo_ref,
     io_ref,
-    trips,
     gints,
+    gsource,
     sints,
     tbuf0,
     tbuf1,
@@ -78,6 +73,8 @@
     atl,
     ohu,
     ohd,
+    uho,
+    dho,
     buy,
     ut,
     dt,
@@ -130,7 +127,6 @@
     yb = (ym, ya, yz)
     slot = c // 2
     pair = c + 1 - 2 * (c % 2)
-    from_pair = 3 - 2 * (c % 2)
     pair_dev = (a, b, pair)
     far_dev = (a, b, (c + 2) % 4)
     sib = (user_index(zhi, y, 1 - core), b, c)
@@ -187,7 +183,6 @@
     for copy in own_tiles:
         copy.start()
     shares = [
-        pltpu.make_async_copy(trip_ref, trips, lsem.at[3]),
         pltpu.make_async_copy(uf_ref, ub.at[0, slot, b], lsem.at[4]),
         pltpu.make_async_copy(if_ref, ib.at[0, zhi, y, core, c], lsem.at[5]),
     ]
@@ -201,18 +196,14 @@
     lanes = lax.broadcasted_iota(jnp.int32, (1, 128), 1)
     source = jnp.full((1, 128), GROUP, jnp.int32)
     for n in range(4 * GROUP):
-        spot = n // GROUP * PLACES + rows_ref[n] // 4 * 8 + cols_ref[n]
-        spot = jnp.where(n < count_ref[0], spot, -1)
-        source = jnp.where(lanes == spot, n % GROUP, source)
-    own = trips[...].T
-    buyers = own[0:1] % 2048
+        source = jnp.where(lanes == spot_ref[n], n % GROUP, source)
+    gsource[0] = source
+    buyers = trip_ref[0:1] % 2048
     gints[0, 0:1] = buyers // 512 * 128 + buyers % 128
     gints[0, 1:2] = buyers // 128 % 4
-    gints[0, 2:3] = own[1:2] // 256 * 64 + own[1:2] % 64
-    gints[0, 3:4] = own[2:3] // 256 * 64 + own[2:3] % 64
-    gints[0, 4:5, 0:128] = source
-    gints[0, 4:5, 128:256] = source
-    gints[0, 5:8] = jnp.zeros((3, 256), jnp.int32)
+    gints[0, 2:3] = trip_ref[1:2] // 256 * 64 + trip_ref[1:2] % 64
+    gints[0, 3:4] = trip_ref[2:3] // 256 * 64 + trip_ref[2:3] % 64
+    gints[0, 4:8] = jnp.zeros((4, 256), jnp.int32)
     count_up = lax.broadcasted_iota(jnp.int32, (256, 256), 0).astype(F32).astype(BF16)
 
     def one_hot(index, m):
@@ -220,15 +211,31 @@
         inside = jnp.broadcast_to(inside, (256, 256)).astype(BF16)
         return jnp.where(count_up == inside, jnp.ones((), BF16), jnp.zeros((), BF16))
 
+    count_right = lax.broadcasted_iota(jnp.int32, (256, 256), 1).astype(F32).astype(BF16)
+
+    def one_hot_rows(index, m):
+        inside = jnp.where(index // 256 == m, index % 256, -1).astype(F32)
+        inside = jnp.broadcast_to(inside, (256, 256)).astype(BF16)
+        return jnp.where(count_right == inside, jnp.ones((), BF16), jnp.zeros((), BF16))
+
     def select_users(k):
         buyers = jnp.where(gints[k, 1:2, :] == c, gints[k, 0:1, :], -1)
+        columns = gints[k].T
+        column = jnp.where(columns[:, 1:2] == c, columns[:, 0:1], -1)
         for m in range(2):
-            ohu[m * 256 : (m + 1) * 256, k * 256 : (k + 1) * 256] = one_hot(buyers, m)
+            block = slice(m * 256, (m + 1) * 256)
+            span = slice(k * 256, (k + 1) * 256)
+            ohu[block, span] = one_hot(buyers, m)
+            uho[span, block] = one_hot_rows(column, m)
 
     def select_items(k):
+        columns = gints[k].T
         for m in range(4):
-            signed = one_hot(gints[k, 2:3, :], m) - one_hot(gints[k, 3:4, :], m)
-            ohd[m * 256 : (m + 1) * 256, k * 256 : (k + 1) * 256] = signed
+            block = slice(m * 256, (m + 1) * 256)
+            span = slice(k * 256, (k + 1) * 256)
+            ohd[block, span] = one_hot(gints[k, 2:3, :], m) - one_hot(gints[k, 3:4, :], m)
+            chosen = one_hot_rows(columns[:, 2:3], m)
+            dho[span, block] = chosen - one_hot_rows(columns[:, 3:4], m)
 
     select_users(0)
     select_items(0)
@@ -458,19 +465,20 @@
             for col in range(8):
                 at_col = slice(col * 128, (col + 1) * 128)
                 spot = (2 * h + c % 2) * PLACES + row * 8 + col
-                tile = tbuf[h][0, sints[0, 4, spot]] + tbuf[h][1, sints[from_pair, 4, spot]]
+                tile = tbuf[h][0, sints[0, 0, spot]] + tbuf[h][1, sints[1, 0, spot]]
                 ah[at_row, at_col], al[at_row, at_col] = split2(tile)
                 ath[at_col, at_row], atl[at_col, at_row] = split2(tile.T)
             return carry
 
         lax.fori_loop(0, 4, place, 0)
 
-    to_scalars = pltpu.make_async_copy(gints, sints, lsem.at[2])
+    to_scalars = pltpu.make_async_copy(gsource, sints, lsem.at[2])
 
     def loss_gradient():
         for k in range(1, 4):
             dev, other = hot_dev(k)
             send(gints.at[0], gints.at[k], INTS + k - 1, dev)
+        send(gsource.at[0], gsource.at[1], SOURCE, pair_dev)
         gather_items_start(0, None)
         gather_users_start(0, None)
         send_tiles(0, EARLY)
@@ -478,6 +486,7 @@
         gather_users_forward(0)
         for k in range(1, 4):
             arrive(gints.at[k], INTS + k - 1, hot_dev(4 - k)[0])
+        arrive(gsource.at[1], SOURCE, pair_dev)
         to_scalars.start()
         gather_items_z(0, NEAR_FIRST[2:])
         for k in range(1, 4):
@@ -487,27 +496,27 @@
             select_items(k)
         gather_items_y(0, NEAR_FIRST[4:])
         gather_users_end(0)
-        ut[0], ut[1], ut[2] = split3(ub[0, slot].reshape(512, 256).T)
+        ut[0], ut[1], ut[2] = split3(ub[0, slot].reshape(512, 256))
         for h in range(4):
             span = slice(h * 256, (h + 1) * 256)
-            hot = ohu[:, span]
-            buy[:, span] = dot(ut[0], hot) + dot(ut[1], hot) + dot(ut[2], hot)
+            hot = uho[span]
+            buy[span] = dot(hot, ut[0]) + dot(hot, ut[1]) + dot(hot, ut[2])
         gather_items_end(0)
-        dt[0], dt[1], dt[2] = split3(ib[0].reshape(1024, 256).T)
+        dt[0], dt[1], dt[2] = split3(ib[0].reshape(1024, 256))
         for h in range(4):
             span = slice(h * 256, (h + 1) * 256)
-            buyer, signed = buy[:, span], ohd[:, span]
-            differ = dot(dt[0], signed) + dot(dt[1], signed) + dot(dt[2], signed)
-            margin = jnp.sum(buyer * differ, axis=0, keepdims=True)
+            buyer, signed = buy[span], dho[span]
+            differ = dot(signed, dt[0]) + dot(signed, dt[1]) + dot(signed, dt[2])
+            margin = jnp.sum(buyer * differ, axis=1, keepdims=True)
             small = jnp.exp(-jnp.abs(margin))
             coef = -jnp.where(margin >= 0, small, 1.0) / (1.0 + small)
-            wu[0, :, span], wu[1, :, span] = split2(coef * buyer)
-            wd[0, :, span], wd[1, :, span] = split2(coef * differ)
+            wu[0, span], wu[1, span] = split2(coef * buyer)
+            wd[0, span], wd[1, span] = split2(coef * differ)
         for m in range(4):
             left = ohd[m * 256 : (m + 1) * 256, :]
-            store_items(0, m, dot_nt(left, wu[0]) + dot_nt(left, wu[1]))
+            store_items(0, m, dot(left, wu[0]) + dot(left, wu[1]))
         scatter_items_core(0)
-        sums = dot_nt(ohu[...], wd[0]) + dot_nt(ohu[...], wd[1])
+        sums = dot(ohu[...], wd[0]) + dot(ohu[...], wd[1])
         pu[0, slot] = sums.reshape(4, 128, 256)
         scatter_users_start(0, 1)
         return scatter(0)
@@ -557,21 +566,24 @@
 
 
 def body(user_final, item_final, tiles, tile_rows, tile_cols, tile_count, triplets):
+    slot = jnp.arange(4 * GROUP, dtype=jnp.int32)
+    spot = slot // GROUP * PLACES + tile_rows // 4 * 8 + tile_cols
+    spot = jnp.where(slot < tile_count[0], spot, -1)
     vmem = pl.BlockSpec(memory_space=pltpu.VMEM)
     smem = pl.BlockSpec(memory_space=pltpu.SMEM)
-    anywhere = pl.BlockSpec(memory_space=pl.ANY)
+    hbm = pl.BlockSpec(memory_space=pltpu.HBM)
     return pl.pallas_call(
         kernel,
         out_shape=(
             jax.ShapeDtypeStruct((128, 256), F32),
             jax.ShapeDtypeStruct((16, 256), F32),
         ),
-        in_specs=[anywhere, smem, smem, smem, anywhere, anywhere, anywhere],
+        in_specs=[vmem, smem, hbm, hbm, hbm],
         out_specs=(vmem, vmem),
         scratch_shapes=[
-            pltpu.VMEM((256, 3), jnp.int32),
             pltpu.VMEM((4, 8, 256), jnp.int32),
-            pltpu.SMEM((4, 8, 256), jnp.int32),
+            pltpu.VMEM((2, 1, 128), jnp.int32),
+            pltpu.SMEM((2, 1, 128), jnp.int32),
             pltpu.VMEM((2, GROUP + 1, 128, 128), F32),
             pltpu.VMEM((2, GROUP + 1, 128, 128), F32),
             pltpu.VMEM((1024, 1024), BF16),
@@ -580,11 +592,13 @@
             pltpu.VMEM((1024, 1024), BF16),
             pltpu.VMEM((512, 1024), BF16),
             pltpu.VMEM((1024, 1024), BF16),
-            pltpu.VMEM((256, 1024), F32),
-            pltpu.VMEM((3, 256, 512), BF16),
-            pltpu.VMEM((3, 256, 1024), BF16),
-            pltpu.VMEM((2, 256, 1024), BF16),
-            pltpu.VMEM((2, 256, 1024), BF16),
+            pltpu.VMEM((1024, 512), BF16),
+            pltpu.VMEM((1024, 1024), BF16),
+            pltpu.VMEM((1024, 256), F32),
+            pltpu.VMEM((3, 512, 256), BF16),
+            pltpu.VMEM((3, 1024, 256), BF16),
+            pltpu.VMEM((2, 1024, 256), BF16),
+            pltpu.VMEM((2, 1024, 256), BF16),
             pltpu.VMEM((ROUNDS, 2, 4, 128, 256), F32),
             pltpu.VMEM((ROUNDS, 2, 4, 2, 4, 16, 256), F32),
             pltpu.VMEM((ROUNDS, 2, 4, 128, 256), F32),
@@ -610,7 +624,7 @@
             collective_id=0, has_side_effects=True, vmem_limit_bytes=52 * 1024 * 1024
         ),
         name="propagate",
-    )(triplets, tile_rows, tile_cols, tile_count, user_final, item_final, tiles)
+    )(triplets.T, spot, user_final, item_final, tiles)
 
 
 def solution(mesh):

time: 130 us -> 130 us (level)
  local copies, waits for them, and re-layouts: 5.01 us -> 3.57 us
    unnamed x11 -> x8, local copies, waits for them, and re-layouts: 5.01 us -> 3.57 us
where the time goes in v6:
time: 130 us; the launch traced here: 129 us
  Pallas kernels  124 us (95%)
  local copies, waits for them, and re-layouts  3.57 us (3%)
  between operations  1.3 us (1%)
    pallas_call x1, Pallas kernels, body(): pl.pallas_call(kernel, out_shape=(jax.ShapeDtypeStruct((128, 256), F32),...  124 us
    unnamed x8, local copies, waits for them, and re-layouts  3.57 us

profile of v6, /device:TPU:1, one launch (start us, length us, event | category | flops | bytes accessed | tf_op | source)
XLA Modules:
  0.0 129.5 jit_solution(3877177129260120011)
XLA Ops:
  1.3 0.7 compare_select_fusion.spot_ref
  2.0 0.0 copy-start
  2.0 0.9 copy-done
  2.9 0.0 copy-start.1
  2.9 0.7 copy-done.1
  3.6 0.0 copy-start.2
  3.6 0.7 copy-done.2
  4.3 123.9 %propagate.1 = (f32[128,256]{1,0:T(8,128)S(1)}, f32[16,256]{1,0:T(8,128)S(1)}) custom-call(s32[3,256]{1,0:T(4,128)S(1)} %bitcast.3, s32[48]{0:T(128)S(1)} %compare_select_fusion.spot_ref, f32[128,256]{1,0:T(8,128)S(1)} %copy-done, f32[16,256]{1,0:T(8,128)S(1)} %copy-done.1, f32[48,128,128]{2,1,0:T(8,128)} %tiles_ref.1), custom_call_target="tpu_custom_call" | custom-call | tf_op jit(solution)/shard_map/propagate/pallas_call | solution.py:575
  128.2 0.7 copy.12
  128.9 0.6 copy.13
Async XLA Ops:
  2.0 0.9 copy-start
  2.9 0.7 copy-start.1
  3.6 0.7 copy-start.2

commit v7 on v6

--- a/solution.py
+++ b/solution.py
@@ -17,9 +17,10 @@
 
 CHUNKS = 4
 CHUNK = 32
-PIECES = 6
-PIECE = 4
-EARLY = 4
+PIECES = 12
+PIECE = 2
+EARLY = 8
+MIDDLE = 10
 
 U_AG = 0
 Z_AG = U_AG + 7 * CHUNKS
@@ -281,18 +282,19 @@
             arrive(block, base + q, xa_dev)
             send(block, block, base + 2 * CHUNKS + q, xb_dev)
 
+    def gather_users_own(r):
+        base = r * PER_ROUND + U_AG
+        for q in range(CHUNKS):
+            arrive(ub.at[r, slot, x2, chunk(q)], base + CHUNKS + q, xb_dev)
+        for q in range(CHUNKS):
+            arrive(ub.at[r, slot, xo, chunk(q)], base + 2 * CHUNKS + q, xb_dev)
+
     def gather_users_end(r):
-        base = r * PER_ROUND + U_AG
-        for q in range(CHUNKS):
-            arrive(ub.at[r, slot, x2, chunk(q)], base + CHUNKS + q, xb_dev)
-        for q in range(CHUNKS):
-            arrive(ub.at[r, slot, xo, chunk(q)], base + 2 * CHUNKS + q, xb_dev)
-        if r:
-            base = base + 3 * CHUNKS
-            for q in range(CHUNKS):
-                arrive(ub.at[r, 1 - slot, x1, chunk(q)], base + q, xa_dev)
-                arrive(ub.at[r, 1 - slot, x2, chunk(q)], base + CHUNKS + q, xb_dev)
-                arrive(ub.at[r, 1 - slot, xo, chunk(q)], base + 2 * CHUNKS + q, xo_dev)
+        base = r * PER_ROUND + U_AG + 3 * CHUNKS
+        for q in range(CHUNKS):
+            arrive(ub.at[r, 1 - slot, x1, chunk(q)], base + q, xa_dev)
+            arrive(ub.at[r, 1 - slot, x2, chunk(q)], base + CHUNKS + q, xb_dev)
+            arrive(ub.at[r, 1 - slot, xo, chunk(q)], base + 2 * CHUNKS + q, xo_dev)
 
     def scatter_users_start(r, own):
         base = r * PER_ROUND + U_RS + 3 * CHUNKS * own
@@ -429,7 +431,7 @@
             scatter_users_sum(r, 0)
         scatter_items_z(r, FAR_FIRST[3:] + (0,))
         if r == 0:
-            send_tiles(EARLY, EARLY + 1)
+            send_tiles(EARLY, MIDDLE)
         users = scatter_users_total(r)
         if r:
             users = gu[...] + users
@@ -446,19 +448,19 @@
 
     def send_tiles(first, last):
         for n in range(first, last):
-            h = n // 3
-            start = (2 * h + 1 - c % 2) * GROUP + n % 3 * PIECE
+            h = n // 6
+            start = (2 * h + 1 - c % 2) * GROUP + n % 6 * PIECE
             send(
                 tiles_ref.at[pl.ds(start, PIECE)],
-                tbuf[h].at[1, pl.ds(n % 3 * PIECE, PIECE)],
+                tbuf[h].at[1, pl.ds(n % 6 * PIECE, PIECE)],
                 TILES + n,
                 pair_dev,
             )
 
     def place_tiles(h):
         own_tiles[h].wait()
-        for n in range(3 * h, 3 * h + 3):
-            arrive(tbuf[h].at[1, pl.ds(n % 3 * PIECE, PIECE)], TILES + n, pair_dev)
+        for n in range(6 * h, 6 * h + 6):
+            arrive(tbuf[h].at[1, pl.ds(n % 6 * PIECE, PIECE)], TILES + n, pair_dev)
 
         def place(row, carry):
             at_row = pl.ds(pl.multiple_of(h * 512 + row * 128, 128), 128)
@@ -495,7 +497,7 @@
         for k in range(1, 4):
             select_items(k)
         gather_items_y(0, NEAR_FIRST[4:])
-        gather_users_end(0)
+        gather_users_own(0)
         ut[0], ut[1], ut[2] = split3(ub[0, slot].reshape(512, 256))
         for h in range(4):
             span = slice(h * 256, (h + 1) * 256)
@@ -521,11 +523,24 @@
         scatter_users_start(0, 1)
         return scatter(0)
 
+    def add_items(r, place, more):
+        uh, ul = split2(ub[r, place].reshape(512, 256))
+        users = pl.ds(pl.multiple_of(place * 512, 512), 512)
+        for m in range(4):
+            rows = slice(m * 256, (m + 1) * 256)
+            high, low = ath[rows, users], atl[rows, users]
+            sums = dot(high, uh) + dot(high, ul) + dot(low, uh)
+            first = 2 * m % 4
+            sums = sums.reshape(2, 2, 64, 256)
+            if more:
+                sums = sums + pi[r, m // 2, first : first + 2]
+            pi[r, m // 2, first : first + 2] = sums
+
     def layer(r, items):
         gather_items_start(r, items)
         gather_users_over_z(r)
         if r == 1:
-            send_tiles(EARLY + 1, PIECES)
+            send_tiles(MIDDLE, PIECES)
         gather_items_z(r, NEAR_FIRST[:2])
         gather_users_forward(r)
         gather_items_z(r, NEAR_FIRST[2:6])
@@ -534,9 +549,11 @@
         gather_items_y(r, (0,) + NEAR_FIRST[:4])
         gather_users_far(r, (2, 3))
         gather_items_y(r, NEAR_FIRST[4:])
-        gather_items_end(r)
         if r == 1:
             place_tiles(1)
+        gather_users_own(r)
+        add_items(r, slot, False)
+        gather_items_end(r)
         xh, xl = split2(ib[r].reshape(1024, 256))
         for own in range(2):
             place = place_of(own)
@@ -545,10 +562,7 @@
             pu[r, place] = sums.reshape(4, 128, 256)
             scatter_users_start(r, own)
         gather_users_end(r)
-        uh, ul = split2(ub[r].reshape(1024, 256))
-        for m in range(4):
-            rows = slice(m * 256, (m + 1) * 256)
-            store_items(r, m, dot(ath[rows], uh) + dot(ath[rows], ul) + dot(atl[rows], uh))
+        add_items(r, 1 - slot, True)
         scatter_items_core(r)
         return scatter(r)
 

time: 130 us -> 132 us (1.015)
  Pallas kernels: 124 us -> 126 us
    pallas_call x1, Pallas kernels: 124 us -> 126 us  [body(): pl.pallas_call(kernel, out_shape=(jax.ShapeDtypeStruct((128, 256), F32),...]
where the time goes in v7:
time: 132 us
  Pallas kernels  126 us (95%)
  local copies, waits for them, and re-layouts  3.57 us (3%)
    pallas_call x1, Pallas kernels, body(): pl.pallas_call(kernel, out_shape=(jax.ShapeDtypeStruct((128, 256), F32),...  126 us
    unnamed x8, local copies, waits for them, and re-layouts  3.57 us

profile of v7, /device:TPU:1, one launch (start us, length us, event | category | flops | bytes accessed | tf_op | source)
XLA Modules:
  0.0 131.7 jit_solution(9014765450465627548)
XLA Ops:
  1.3 0.7 compare_select_fusion.spot_ref
  2.0 0.0 copy-start
  2.0 0.9 copy-done
  2.9 0.0 copy-start.1
  2.9 0.7 copy-done.1
  3.6 0.0 copy-start.2
  3.6 0.7 copy-done.2
  4.3 126.2 %propagate.1 = (f32[128,256]{1,0:T(8,128)S(1)}, f32[16,256]{1,0:T(8,128)S(1)}) custom-call(s32[3,256]{1,0:T(4,128)S(1)} %bitcast.3, s32[48]{0:T(128)S(1)} %compare_select_fusion.spot_ref, f32[128,256]{1,0:T(8,128)S(1)} %copy-done, f32[16,256]{1,0:T(8,128)S(1)} %copy-done.1, f32[48,128,128]{2,1,0:T(8,128)} %tiles_ref.1), custom_call_target="tpu_custom_call" | custom-call | tf_op jit(solution)/shard_map/propagate/pallas_call | solution.py:589
  130.5 0.7 copy.12
  131.1 0.6 copy.13
Async XLA Ops:
  2.0 0.9 copy-start
  2.9 0.7 copy-start.1
  3.6 0.7 copy-start.2

commit v8 on v6

--- a/solution.py
+++ b/solution.py
@@ -17,9 +17,10 @@
 
 CHUNKS = 4
 CHUNK = 32
-PIECES = 6
-PIECE = 4
-EARLY = 4
+PIECES = 12
+PIECE = 2
+EARLY = 8
+MIDDLE = 10
 
 U_AG = 0
 Z_AG = U_AG + 7 * CHUNKS
@@ -429,7 +430,7 @@
             scatter_users_sum(r, 0)
         scatter_items_z(r, FAR_FIRST[3:] + (0,))
         if r == 0:
-            send_tiles(EARLY, EARLY + 1)
+            send_tiles(EARLY, MIDDLE)
         users = scatter_users_total(r)
         if r:
             users = gu[...] + users
@@ -446,19 +447,19 @@
 
     def send_tiles(first, last):
         for n in range(first, last):
-            h = n // 3
-            start = (2 * h + 1 - c % 2) * GROUP + n % 3 * PIECE
+            h = n // 6
+            start = (2 * h + 1 - c % 2) * GROUP + n % 6 * PIECE
             send(
                 tiles_ref.at[pl.ds(start, PIECE)],
-                tbuf[h].at[1, pl.ds(n % 3 * PIECE, PIECE)],
+                tbuf[h].at[1, pl.ds(n % 6 * PIECE, PIECE)],
                 TILES + n,
                 pair_dev,
             )
 
     def place_tiles(h):
         own_tiles[h].wait()
-        for n in range(3 * h, 3 * h + 3):
-            arrive(tbuf[h].at[1, pl.ds(n % 3 * PIECE, PIECE)], TILES + n, pair_dev)
+        for n in range(6 * h, 6 * h + 6):
+            arrive(tbuf[h].at[1, pl.ds(n % 6 * PIECE, PIECE)], TILES + n, pair_dev)
 
         def place(row, carry):
             at_row = pl.ds(pl.multiple_of(h * 512 + row * 128, 128), 128)
@@ -525,7 +526,7 @@
         gather_items_start(r, items)
         gather_users_over_z(r)
         if r == 1:
-            send_tiles(EARLY + 1, PIECES)
+            send_tiles(MIDDLE, PIECES)
         gather_items_z(r, NEAR_FIRST[:2])
         gather_users_forward(r)
         gather_items_z(r, NEAR_FIRST[2:6])
@@ -533,10 +534,10 @@
         gather_items_z(r, NEAR_FIRST[6:])
         gather_items_y(r, (0,) + NEAR_FIRST[:4])
         gather_users_far(r, (2, 3))
+        if r == 1:
+            place_tiles(1)
         gather_items_y(r, NEAR_FIRST[4:])
         gather_items_end(r)
-        if r == 1:
-            place_tiles(1)
         xh, xl = split2(ib[r].reshape(1024, 256))
         for own in range(2):
             place = place_of(own)

time: 130 us -> 129 us (level)
  no operation moved by 1% of the time
where the time goes in v8:
time: 129 us
  Pallas kernels  123 us (95%)
  local copies, waits for them, and re-layouts  3.57 us (3%)
  between operations  1.3 us (1%)
    pallas_call x1, Pallas kernels, body(): pl.pallas_call(kernel, out_shape=(jax.ShapeDtypeStruct((128, 256), F32),...  123 us
    unnamed x8, local copies, waits for them, and re-layouts  3.57 us

profile of v8, /device:TPU:1, one launch (start us, length us, event | category | flops | bytes accessed | tf_op | source)
XLA Modules:
  0.0 128.8 jit_solution(5945554694331992556)
XLA Ops:
  1.3 0.7 compare_select_fusion.spot_ref
  2.0 0.0 copy-start
  2.0 0.9 copy-done
  2.9 0.0 copy-start.1
  2.9 0.7 copy-done.1
  3.6 0.0 copy-start.2
  3.6 0.7 copy-done.2
  4.3 123.3 %propagate.1 = (f32[128,256]{1,0:T(8,128)S(1)}, f32[16,256]{1,0:T(8,128)S(1)}) custom-call(s32[3,256]{1,0:T(4,128)S(1)} %bitcast.3, s32[48]{0:T(128)S(1)} %compare_select_fusion.spot_ref, f32[128,256]{1,0:T(8,128)S(1)} %copy-done, f32[16,256]{1,0:T(8,128)S(1)} %copy-done.1, f32[48,128,128]{2,1,0:T(8,128)} %tiles_ref.1), custom_call_target="tpu_custom_call" | custom-call | tf_op jit(solution)/shard_map/propagate/pallas_call | solution.py:576
  127.6 0.7 copy.12
  128.2 0.6 copy.13
Async XLA Ops:
  2.0 0.9 copy-start
  2.9 0.7 copy-start.1
  3.6 0.7 copy-start.2
